TPU v7x, 32 devices: a whole 2x2x4 slice. The times are simulated.
32 devices in a mesh: sy: 4 (over x, core), sx: 4 (over z), ch: 2 (over y).
Axes of the slice: x: 2, y: 2, z: 4, core: 2. Of those that a mesh axis runs over, the one named last changes fastest.
Arguments:
- frames: bfloat16 [144, 144, 128], P('sy', 'sx'), may hold values from -6 to 6
- w_input: bfloat16 [9, 64, 4, 1024], P(None, None, None, 'ch'), may hold values from -0.25 to 0.25
- w_hidden: bfloat16 [9, 1024, 4, 1024], P(None, None, None, 'ch'), may hold values from -0.0625 to 0.0625
- biases: float32 [4, 1024], P(None, 'ch'), may hold values from -4 to 4
- hidden_init: bfloat16 [144, 144, 1024], P('sy', 'sx', 'ch'), may hold values from -1 to 1
- cell_init: float32 [144, 144, 1024], P('sy', 'sx', 'ch'), may hold values from -5 to 5
Outputs:
- hidden_out: bfloat16 [144, 144, 1024], P('sy', 'sx', 'ch')
- cell_out: float32 [144, 144, 1024], P('sy', 'sx', 'ch')
All inputs are finite; a program needn't handle non-finite values.
Results may differ from a plain program's by a relative error of at most 0.0021.
Values may be sent and summed in bfloat16 or wider, within the bound.
No kernel may reach another device: no remote copies, remote signals or barrier semaphores. Data moves between devices by JAX's collectives and lax.ppermute only.
A program may use at most 448 MiB of HBM per device.

v0:
```python
import jax
import jax.numpy as jnp
from jax import lax
from jax.sharding import PartitionSpec as P

STEPS = 2


def with_halo(cells, sides, width):
    for axis, dim in sides:
        count = lax.axis_size(axis)
        ends = count - 1
        head = lax.slice_in_dim(cells, 0, width, axis=dim)
        tail = lax.slice_in_dim(cells, cells.shape[dim] - width, cells.shape[dim], axis=dim)
        cells = jnp.concatenate(
            [
                lax.ppermute(tail, axis, [(i, (i + 1) % count) for i in range(ends)]),
                cells,
                lax.ppermute(head, axis, [((i + 1) % count, i) for i in range(ends)]),
            ],
            axis=dim,
        )
    return cells


def taps_sum(padded, kernels, rows, cols, total):
    for tap in range(9):
        offset_y = tap // 3
        offset_x = tap % 3
        window = padded[offset_y : offset_y + rows, offset_x : offset_x + cols]
        window = window.reshape(rows * cols, window.shape[2])
        total = total + jnp.dot(window, kernels[tap], preferred_element_type=jnp.float32)
    return total


def per_device(frames, w_input, w_hidden, biases, hidden_init, cell_init):
    rows, cols, width = hidden_init.shape
    in_kernels = w_input.reshape(9, w_input.shape[1], 4 * width)
    hid_kernels = w_hidden.reshape(9, w_hidden.shape[1], 4 * width)
    in_width = frames.shape[2] // STEPS
    framed = with_halo(frames, (("sy", 0), ("sx", 1)), 1)
    bias_row = biases.reshape(1, 4 * width)
    hidden = hidden_init
    cell = cell_init
    for step in range(STEPS):
        frame = framed[:, :, step * in_width : (step + 1) * in_width]
        start_sum = jnp.zeros((rows * cols, 4 * width), jnp.float32) + bias_row
        total = taps_sum(frame, in_kernels, rows, cols, start_sum)
        whole = lax.all_gather(hidden, "ch", axis=2, tiled=True)
        padded = with_halo(whole, (("sy", 0), ("sx", 1)), 1)
        total = taps_sum(padded, hid_kernels, rows, cols, total)
        gates = total.reshape(rows, cols, 4, width)
        cell = jax.nn.sigmoid(gates[:, :, 1]) * cell + jax.nn.sigmoid(gates[:, :, 0]) * jnp.tanh(
            gates[:, :, 3]
        )
        hidden = (jax.nn.sigmoid(gates[:, :, 2]) * jnp.tanh(cell)).astype(jnp.bfloat16)
    return (hidden, cell)


def solution(mesh):
    in_specs = (
        P("sy", "sx", None),
        P(None, None, None, "ch"),
        P(None, None, None, "ch"),
        P(None, "ch"),
        P("sy", "sx", "ch"),
        P("sy", "sx", "ch"),
    )
    out_specs = (P("sy", "sx", "ch"), P("sy", "sx", "ch"))
    return jax.shard_map(
        per_device, mesh=mesh, in_specs=in_specs, out_specs=out_specs, check_vma=False
    )
```

profile of v0, /device:TPU:0, one launch (start us, length us, event | category | flops | bytes accessed | tf_op | source)
XLA Modules:
  0.0 709.2 jit_solution(4614158183443708209)
XLA Ops:
  13.6 27.6 %fusion.54 = (bf16[1,1024,4,512]{3,2,1,0:T(4,128)(2,1)}, bf16[1,1024,4,512]{3,2,1,0:T(4,128)(2,1)}, bf16[1,1024,4,512]{3,2,1,0:T(4,128)(2,1)}, bf16[1,1024,4,512...) fusion(bf16[9,1024,4,512]{3,2,1,0:T(4,128)(2,1)} %param.8), kind=kLoop, calls=%fused_computation.103 | loop fusion | bytes 75497472 | tf_op jit(solution)/shard_map/slice | solution.py:32
  43.2 5.5 fusion.80
  48.7 5.5 fusion.71
  71.6 3.5 copy.82
  75.1 3.5 copy.88
  86.3 6.2 collective-permute-start.2
  100.3 5.5 fusion.83
  105.8 5.5 fusion.74
  112.3 5.5 fusion.77
  117.9 5.4 fusion.68
  126.9 5.4 fusion.76
  139.6 5.4 fusion.78
  145.0 5.9 fusion.79
  150.9 5.4 fusion.81
  156.4 5.4 fusion.82
  161.8 5.5 fusion.84
  172.2 3.5 reshape.218
  175.7 10.5 %fusion.89 = f32[1296,2048]{1,0:T(8,128)} fusion(bf16[1296,1024]{1,0:T(8,128)(2,1)S(1)} %reshape.218, bf16[1024,2048]{1,0:T(8,128)(2,1)} %bitcast.189), kind=kOutput, calls=%fused_computation.138 | convolution fusion | flops 5435817984 | bytes 17465344 | tf_op jit(solution)/shard_map/dot_general | solution.py:32
  190.8 4.3 collective-permute-start.6
  196.6 4.9 reshape.215
  203.6 10.8 %fusion.86 = f32[1296,2048]{1,0:T(8,128)} fusion(bf16[1296,1024]{1,0:T(8,128)(2,1)} %reshape.215, bf16[1024,2048]{1,0:T(8,128)(2,1)} %bitcast.187), kind=kOutput, calls=%fused_computation.135 | convolution fusion | flops 5435817984 | bytes 17465344 | tf_op jit(solution)/shard_map/dot_general | solution.py:32
  214.4 8.3 %fusion.92 = f32[1296,2048]{1,0:T(8,128)} fusion(bf16[1296,1024]{1,0:T(8,128)(2,1)S(1)} %copy-done.28, bf16[1024,2048]{1,0:T(8,128)(2,1)S(1)} %bitcast.186), kind=kOutput, calls=%fused_computation.141 | convolution fusion | flops 5435817984 | bytes 17465344 | tf_op jit(solution)/shard_map/dot_general | solution.py:32
  223.0 9.3 %fusion.7 = (bf16[36,36,1024]{2,1,0:T(8,128)(2,1)}, bf16[36,36,1024]{2,1,0:T(8,128)(2,1)}, bf16[36,36,1024]{2,1,0:T(8,128)(2,1)}, bf16[36,36,1024]{2,1,0:T(8,128...) fusion(bf16[38,1,1024]{2,1,0:T(2,128)(2,1)S(1)} %copy.52, ...), kind=kLoop, calls=%fused_computation.17 | loop fusion | flops 31850496 | bytes 18882560 | tf_op jit(solution)/shard_map/concatenate | solution.py:15
  232.4 4.9 reshape.214
  237.3 4.9 reshape.216
  242.2 4.9 reshape.217
  247.1 4.9 reshape.219
  252.0 4.9 reshape.220
  259.1 10.9 %fusion.85 = f32[1296,2048]{1,0:T(8,128)} fusion(bf16[1296,1024]{1,0:T(8,128)(2,1)} %reshape.214, bf16[1024,2048]{1,0:T(8,128)(2,1)} %bitcast.183), kind=kOutput, calls=%fused_computation.134 | convolution fusion | flops 5435817984 | bytes 17465344 | tf_op jit(solution)/shard_map/dot_general | solution.py:32
  270.0 8.7 %fusion.87 = f32[1296,2048]{1,0:T(8,128)} fusion(bf16[1296,1024]{1,0:T(8,128)(2,1)S(1)} %copy-done.24, bf16[1024,2048]{1,0:T(8,128)(2,1)S(1)} %bitcast.182), kind=kOutput, calls=%fused_computation.136 | convolution fusion | flops 5435817984 | bytes 17465344 | tf_op jit(solution)/shard_map/dot_general | solution.py:32
  278.7 8.3 %fusion.88 = f32[1296,2048]{1,0:T(8,128)} fusion(bf16[1296,1024]{1,0:T(8,128)(2,1)S(1)} %copy-done.25, bf16[1024,2048]{1,0:T(8,128)(2,1)S(1)} %bitcast.180), kind=kOutput, calls=%fused_computation.137 | convolution fusion | flops 5435817984 | bytes 17465344 | tf_op jit(solution)/shard_map/dot_general | solution.py:32
  287.0 8.2 %fusion.90 = f32[1296,2048]{1,0:T(8,128)} fusion(bf16[1296,1024]{1,0:T(8,128)(2,1)S(1)} %copy-done.26, bf16[1024,2048]{1,0:T(8,128)(2,1)S(1)} %bitcast.178), kind=kOutput, calls=%fused_computation.139 | convolution fusion | flops 5435817984 | bytes 17465344 | tf_op jit(solution)/shard_map/dot_general | solution.py:32
  295.2 8.3 %fusion.91 = f32[1296,2048]{1,0:T(8,128)} fusion(bf16[1296,1024]{1,0:T(8,128)(2,1)S(1)} %copy-done.27, bf16[1024,2048]{1,0:T(8,128)(2,1)S(1)} %bitcast.176), kind=kOutput, calls=%fused_computation.140 | convolution fusion | flops 5435817984 | bytes 17465344 | tf_op jit(solution)/shard_map/dot_general | solution.py:32
  303.6 61.0 %add_add_fusion.1 = f32[1296,2048]{1,0:T(8,128)} fusion(f32[1296,2048]{1,0:T(8,128)} %fusion.92, f32[1296,2048]{1,0:T(8,128)} %fusion.91, f32[1296,2048]{1,0:T(8,128)} %fusion.90, f32[1296,2048]{1,0:T(8,128)} %fusion.89, f32[1296,2048]{1,0:T(8,128)} %fusion.88, f32[1296,2048]{1,0:T(8,128)} %fusion.87, f32[1296,2048]{1,0:T(8,128)} %fusion.86, ...), kind=kOutput, calls=%fused_computation.1 | convolution fusion | flops 5483593728 | bytes 197959680 | tf_op jit(solution)/shard_map/dot_general | solution.py:32
  364.5 13.5 %reshape.223 = f32[36,36,4,512]{3,2,1,0:T(4,128)} reshape(f32[1296,2048]{1,0:T(8,128)} %add_add_fusion.1) | data formatting | bytes 21233664 | tf_op jit(solution)/shard_map/reshape | solution.py:52
  378.0 24.4 %fusion.56 = (f32[36,36,1,512]{3,2,1,0:T(1,128)S(1)}, f32[36,36,1,512]{3,2,1,0:T(1,128)S(1)}, f32[36,36,1,512]{3,2,1,0:T(1,128)S(1)}, f32[36,36,1,512]{3,2,1,0:T(1,128)S(1)}) fusion(f32[36,36,4,512]{3,2,1,0:T(4,128)} %reshape.223), kind=kLoop, calls=%fused_computation.105 | loop fusion | bytes 21233664 | tf_op jit(solution)/shard_map/slice | solution.py:53
  402.4 4.5 fusion.40
  407.0 5.5 fusion.67
  413.2 5.6 fusion.69
  418.8 5.6 fusion.70
  424.4 5.4 fusion.72
  429.8 5.6 fusion.73
  435.3 5.4 fusion.75
  440.7 13.9 %all-gather.5.cloned.1.call-done = bf16[36,36,1024]{2,1,0:T(8,128)(2,1)} async-done(((bf16[36,36,512]{2,1,0:T(8,128)(2,1)}), bf16[36,36,1024]{2,1,0:T(8,128)(2,1)}) %all-gather.5.cloned.1.call-update) | async-done | bytes 2654224 | tf_op jit(solution)/shard_map/all_gather | solution.py:49
  458.7 3.9 reshape.228
  462.6 10.6 %fusion.97 = f32[1296,2048]{1,0:T(8,128)} fusion(bf16[1296,1024]{1,0:T(8,128)(2,1)S(1)} %reshape.228, bf16[1024,2048]{1,0:T(8,128)(2,1)} %bitcast.190), kind=kOutput, calls=%fused_computation.146 | convolution fusion | flops 5435817984 | bytes 17465344 | tf_op jit(solution)/shard_map/dot_general | solution.py:32
  483.1 4.9 reshape.225
  488.0 10.7 %fusion.94 = f32[1296,2048]{1,0:T(8,128)} fusion(bf16[1296,1024]{1,0:T(8,128)(2,1)} %reshape.225, bf16[1024,2048]{1,0:T(8,128)(2,1)} %bitcast.188), kind=kOutput, calls=%fused_computation.143 | convolution fusion | flops 5435817984 | bytes 17465344 | tf_op jit(solution)/shard_map/dot_general | solution.py:32
  500.9 10.8 %fusion.100 = f32[1296,2048]{1,0:T(8,128)} fusion(bf16[1296,1024]{1,0:T(8,128)(2,1)} %reshape.231, bf16[1024,2048]{1,0:T(8,128)(2,1)} %bitcast.185), kind=kOutput, calls=%fused_computation.149 | convolution fusion | flops 5435817984 | bytes 17465344 | tf_op jit(solution)/shard_map/dot_general | solution.py:32
  511.6 9.3 %fusion.3 = (bf16[36,36,1024]{2,1,0:T(8,128)(2,1)}, bf16[36,36,1024]{2,1,0:T(8,128)(2,1)S(1)}, bf16[36,36,1024]{2,1,0:T(8,128)(2,1)}, bf16[36,36,1024]{2,1,0:T(8...) fusion(bf16[38,1,1024]{2,1,0:T(2,128)(2,1)S(1)} %collective-permute-done.10, ...), kind=kLoop, calls=%fused_computation.13 | loop fusion | flops 31850496 | bytes 18882560 | tf_op jit(solution)/shard_map/concatenate | solution.py:15
  521.0 4.9 reshape.224
  525.9 10.6 %fusion.93 = f32[1296,2048]{1,0:T(8,128)} fusion(bf16[1296,1024]{1,0:T(8,128)(2,1)} %reshape.224, bf16[1024,2048]{1,0:T(8,128)(2,1)} %bitcast.184), kind=kOutput, calls=%fused_computation.142 | convolution fusion | flops 5435817984 | bytes 17465344 | tf_op jit(solution)/shard_map/dot_general | solution.py:32
  536.5 4.9 reshape.226
  541.4 10.8 %fusion.95 = f32[1296,2048]{1,0:T(8,128)} fusion(bf16[1296,1024]{1,0:T(8,128)(2,1)} %reshape.226, bf16[1024,2048]{1,0:T(8,128)(2,1)} %bitcast.181), kind=kOutput, calls=%fused_computation.144 | convolution fusion | flops 5435817984 | bytes 17465344 | tf_op jit(solution)/shard_map/dot_general | solution.py:32
  552.2 4.9 reshape.227
  557.1 10.7 %fusion.96 = f32[1296,2048]{1,0:T(8,128)} fusion(bf16[1296,1024]{1,0:T(8,128)(2,1)} %reshape.227, bf16[1024,2048]{1,0:T(8,128)(2,1)} %bitcast.179), kind=kOutput, calls=%fused_computation.145 | convolution fusion | flops 5435817984 | bytes 17465344 | tf_op jit(solution)/shard_map/dot_general | solution.py:32
  567.8 4.9 reshape.229
  572.7 10.7 %fusion.98 = f32[1296,2048]{1,0:T(8,128)} fusion(bf16[1296,1024]{1,0:T(8,128)(2,1)} %reshape.229, bf16[1024,2048]{1,0:T(8,128)(2,1)} %bitcast.177), kind=kOutput, calls=%fused_computation.147 | convolution fusion | flops 5435817984 | bytes 17465344 | tf_op jit(solution)/shard_map/dot_general | solution.py:32
  585.6 10.7 %fusion.99 = f32[1296,2048]{1,0:T(8,128)} fusion(bf16[1296,1024]{1,0:T(8,128)(2,1)} %reshape.230, bf16[1024,2048]{1,0:T(8,128)(2,1)} %bitcast.175), kind=kOutput, calls=%fused_computation.148 | convolution fusion | flops 5435817984 | bytes 17465344 | tf_op jit(solution)/shard_map/dot_general | solution.py:32
  596.3 3.5 reshape.232
  599.8 59.8 %add_add_fusion = f32[1296,2048]{1,0:T(8,128)} fusion(f32[1296,2048]{1,0:T(8,128)} %fusion.100, f32[1296,2048]{1,0:T(8,128)} %fusion.99, f32[1296,2048]{1,0:T(8,128)} %fusion.98, f32[1296,2048]{1,0:T(8,128)} %fusion.97, f32[1296,2048]{1,0:T(8,128)} %fusion.96, f32[1296,2048]{1,0:T(8,128)} %fusion.95, f32[1296,2048]{1,0:T(8,128)} %fusion.94, ...), kind=kOutput, calls=%fused_computation | convolution fusion | flops 5483593728 | bytes 197959680 | tf_op jit(solution)/shard_map/dot_general | solution.py:32
  659.6 13.6 %reshape.233 = f32[36,36,4,512]{3,2,1,0:T(4,128)} reshape(f32[1296,2048]{1,0:T(8,128)} %add_add_fusion) | data formatting | bytes 21233664 | tf_op jit(solution)/shard_map/reshape | solution.py:52
  673.2 24.4 %fusion.55 = (f32[36,36,1,512]{3,2,1,0:T(1,128)S(1)}, f32[36,36,1,512]{3,2,1,0:T(1,128)S(1)}, f32[36,36,1,512]{3,2,1,0:T(1,128)S(1)}, f32[36,36,1,512]{3,2,1,0:T(1,128)S(1)}) fusion(f32[36,36,4,512]{3,2,1,0:T(4,128)} %reshape.233), kind=kLoop, calls=%fused_computation.104 | loop fusion | bytes 21233664 | tf_op jit(solution)/shard_map/slice | solution.py:53
  697.7 4.5 fusion.41
  (199 shorter events, 87.3 us)
Async XLA Ops:
  7.2 160.1 %all-gather.3.cloned.1.call-start = ((), (), s32[]{:S(2)}) async-start(), calls=%async_computation | async-start | bytes 4423680 | tf_op jit(solution)/shard_map/all_gather | solution.py:49
  7.9 446.8 %all-gather.5.cloned.1.call-start = ((), (), s32[]{:S(2)}) async-start(), calls=%async_computation.1 | async-start | bytes 4423680 | tf_op jit(solution)/shard_map/all_gather | solution.py:49
  8.7 77.3 %collective-permute-start = (bf16[1,36,128]{2,1,0:T(8,128)(2,1)S(1)}, bf16[1,36,128]{2,1,0:T(8,128)(2,1)S(1)}, u32[]{:S(2)}, u32[]{:S(2)}) collective-permute-start(bf16[1,36,128]{2,1,0:T(8,128)(2,1)S(1)} %get-tuple-element.88), channel_id=1, source_target_pairs={{0,8},{8,16},{16,24},{1,9},{9,17},{17,25},{2,10},{10,18},{18,26},{... | collective-permute-start | bytes 27656 | tf_op jit(solution)/shard_map/ppermute | solution.py:17
  11.0 75.2 %collective-permute-start.1 = (bf16[1,36,128]{2,1,0:T(8,128)(2,1)S(1)}, bf16[1,36,128]{2,1,0:T(8,128)(2,1)S(1)}, u32[]{:S(2)}, u32[]{:S(2)}) collective-permute-start(bf16[1,36,128]{2,1,0:T(8,128)(2,1)S(1)} %get-tuple-element.87), channel_id=1, source_target_pairs={{8,0},{16,8},{24,16},{9,1},{17,9},{25,17},{10,2},{18,10},{26,18},{... | collective-permute-start | bytes 27656 | tf_op jit(solution)/shard_map/ppermute | solution.py:19
  13.6 27.7 %copy-start.41 = (bf16[9,64,4,512]{3,2,1,0:T(4,128)(2,1)S(1)}, bf16[9,64,4,512]{3,2,1,0:T(4,128)(2,1)}, u32[]{:S(2)}) copy-start(bf16[9,64,4,512]{3,2,1,0:T(4,128)(2,1)} %param.7) | copy-start | bytes 7077892
  48.7 5.5 copy-start.9
  54.3 3.4 copy-start.8
  57.6 3.4 copy-start.7
  61.0 3.4 copy-start.6
  64.4 3.4 copy-start.5
  67.8 3.4 copy-start.50
  67.8 3.5 copy-start.49
  67.8 3.8 copy-start.4
  71.2 55.7 %copy-start.39 = (bf16[8,8,4,512]{3,1,2,0:T(8,128)(2,1)}, bf16[8,8,4,512]{3,1,2,0:T(8,128)(2,1)S(1)}, u32[]{:S(2)}) copy-start(bf16[8,8,4,512]{3,1,2,0:T(8,128)(2,1)S(1)} %copy.72) | copy-start | bytes 786436
  71.3 68.3 %copy-start.37 = (bf16[8,8,4,512]{3,1,2,0:T(8,128)(2,1)}, bf16[8,8,4,512]{3,1,2,0:T(8,128)(2,1)S(1)}, u32[]{:S(2)}) copy-start(bf16[8,8,4,512]{3,1,2,0:T(8,128)(2,1)S(1)} %copy.74) | copy-start | bytes 786436
  71.4 73.6 %copy-start.35 = (bf16[8,8,4,512]{3,1,2,0:T(8,128)(2,1)}, bf16[8,8,4,512]{3,1,2,0:T(8,128)(2,1)S(1)}, u32[]{:S(2)}) copy-start(bf16[8,8,4,512]{3,1,2,0:T(8,128)(2,1)S(1)} %copy.75) | copy-start | bytes 786436
  71.4 79.5 %copy-start.33 = (bf16[8,8,4,512]{3,1,2,0:T(8,128)(2,1)}, bf16[8,8,4,512]{3,1,2,0:T(8,128)(2,1)S(1)}, u32[]{:S(2)}) copy-start(bf16[8,8,4,512]{3,1,2,0:T(8,128)(2,1)S(1)} %copy.77) | copy-start | bytes 786436
  71.5 84.9 %copy-start.31 = (bf16[8,8,4,512]{3,1,2,0:T(8,128)(2,1)}, bf16[8,8,4,512]{3,1,2,0:T(8,128)(2,1)S(1)}, u32[]{:S(2)}) copy-start(bf16[8,8,4,512]{3,1,2,0:T(8,128)(2,1)S(1)} %copy.78) | copy-start | bytes 786436
  71.6 90.2 %copy-start.29 = (bf16[8,8,4,512]{3,1,2,0:T(8,128)(2,1)}, bf16[8,8,4,512]{3,1,2,0:T(8,128)(2,1)S(1)}, u32[]{:S(2)}) copy-start(bf16[8,8,4,512]{3,1,2,0:T(8,128)(2,1)S(1)} %copy.80) | copy-start | bytes 786436
  71.6 3.5 copy-start.3
  75.1 3.6 copy-start.2
  82.1 3.9 copy-start.22
  86.2 8.6 %copy-start.43 = (bf16[37,36,128]{2,1,0:T(8,128)(2,1)}, bf16[37,36,128]{2,1,0:T(8,128)(2,1)S(1)}, u32[]{:S(2)}) copy-start(bf16[37,36,128]{2,1,0:T(8,128)(2,1)S(1)} %get-tuple-element.84) | copy-start | bytes 1022980
  86.3 37.0 %collective-permute-start.2 = (bf16[38,1,128]{2,1,0:T(2,128)(2,1)S(1)}, bf16[38,1,128]{2,1,0:T(2,128)(2,1)}, u32[]{:S(2)}, u32[]{:S(2)}) collective-permute-start(bf16[38,1,128]{2,1,0:T(2,128)(2,1)S(1)} %get-tuple-element.76), channel_id=1, source_target_pairs={{0,2},{2,4},{4,6},{1,3},{3,5},{5,7},{8,10},{10,12},{12,14},{9,11},... | collective-permute-start | bytes 29192 | tf_op jit(solution)/shard_map/ppermute | solution.py:17
  92.5 39.8 %collective-permute-start.3 = (bf16[38,1,128]{2,1,0:T(2,128)(2,1)S(1)}, bf16[38,1,128]{2,1,0:T(2,128)(2,1)S(1)}, u32[]{:S(2)}, u32[]{:S(2)}) collective-permute-start(bf16[38,1,128]{2,1,0:T(2,128)(2,1)S(1)} %get-tuple-element.77), channel_id=1, source_target_pairs={{2,0},{4,2},{6,4},{3,1},{5,3},{7,5},{10,8},{12,10},{14,12},{11,9},... | collective-permute-start | bytes 29192 | tf_op jit(solution)/shard_map/ppermute | solution.py:19
  168.2 18.0 %collective-permute-start.4 = (bf16[1,36,1024]{2,1,0:T(8,128)(2,1)S(1)}, bf16[1,36,1024]{2,1,0:T(8,128)(2,1)S(1)}, u32[]{:S(2)}, u32[]{:S(2)}) collective-permute-start(bf16[1,36,1024]{2,1,0:T(8,128)(2,1)S(1)} %get-tuple-element.54), channel_id=1, source_target_pairs={{0,8},{8,16},{16,24},{1,9},{9,17},{17,25},{2,10},{10,18},{18,26},{... | collective-permute-start | bytes 221192 | tf_op jit(solution)/shard_map/ppermute | solution.py:17
  170.9 15.4 %collective-permute-start.5 = (bf16[1,36,1024]{2,1,0:T(8,128)(2,1)S(1)}, bf16[1,36,1024]{2,1,0:T(8,128)(2,1)S(1)}, u32[]{:S(2)}, u32[]{:S(2)}) collective-permute-start(bf16[1,36,1024]{2,1,0:T(8,128)(2,1)S(1)} %get-tuple-element.53), channel_id=1, source_target_pairs={{8,0},{16,8},{24,16},{9,1},{17,9},{25,17},{10,2},{18,10},{26,18},{... | collective-permute-start | bytes 221192 | tf_op jit(solution)/shard_map/ppermute | solution.py:19
  175.7 10.5 %copy-start.10 = (bf16[36,36,1024]{2,1,0:T(8,128)(2,1)S(1)}, bf16[36,36,1024]{2,1,0:T(8,128)(2,1)}, u32[]{:S(2)}) copy-start(bf16[36,36,1024]{2,1,0:T(8,128)(2,1)} %all-gather.3.cloned.1.call-done) | copy-start | bytes 7962628
  190.8 32.0 %collective-permute-start.6 = (bf16[38,1,1024]{2,0,1:T(8,128)(2,1)S(1)}, bf16[38,1,1024]{2,0,1:T(8,128)(2,1)S(1)}, u32[]{:S(2)}, u32[]{:S(2)}) collective-permute-start(bf16[38,1,1024]{2,0,1:T(8,128)(2,1)S(1)} %copy.51), channel_id=1, source_target_pairs={{0,2},{2,4},{4,6},{1,3},{3,5},{5,7},{8,10},{10,12},{12,14},{9,11},... | collective-permute-start | bytes 233480 | tf_op jit(solution)/shard_map/ppermute | solution.py:17
  195.1 27.8 %collective-permute-start.7 = (bf16[38,1,1024]{2,0,1:T(8,128)(2,1)S(1)}, bf16[38,1,1024]{2,0,1:T(8,128)(2,1)S(1)}, u32[]{:S(2)}, u32[]{:S(2)}) collective-permute-start(bf16[38,1,1024]{2,0,1:T(8,128)(2,1)S(1)} %copy.53), channel_id=1, source_target_pairs={{2,0},{4,2},{6,4},{3,1},{5,3},{7,5},{10,8},{12,10},{14,12},{11,9},... | collective-permute-start | bytes 233480 | tf_op jit(solution)/shard_map/ppermute | solution.py:19
  203.6 10.8 %copy-start.17 = (bf16[128,8,4,512]{3,1,2,0:T(8,128)(2,1)S(1)}, bf16[128,8,4,512]{3,1,2,0:T(8,128)(2,1)}, u32[]{:S(2)}) copy-start(bf16[128,8,4,512]{3,1,2,0:T(8,128)(2,1)} %copy.88) | copy-start | bytes 12582916
  203.6 10.8 %copy-start.28 = (bf16[1296,1024]{1,0:T(8,128)(2,1)S(1)}, bf16[1296,1024]{1,0:T(8,128)(2,1)}, u32[]{:S(2)}) copy-start(bf16[1296,1024]{1,0:T(8,128)(2,1)} %reshape.221) | copy-start | bytes 7962628
  214.4 8.6 %copy-start.19 = (bf16[38,36,1024]{2,1,0:T(8,128)(2,1)S(1)}, bf16[38,36,1024]{2,1,0:T(8,128)(2,1)}, u32[]{:S(2)}) copy-start(bf16[38,36,1024]{2,1,0:T(8,128)(2,1)} %copy-done.18) | copy-start | bytes 8404996
  259.1 10.9 %copy-start.16 = (bf16[128,8,4,512]{3,1,2,0:T(8,128)(2,1)S(1)}, bf16[128,8,4,512]{3,1,2,0:T(8,128)(2,1)}, u32[]{:S(2)}) copy-start(bf16[128,8,4,512]{3,1,2,0:T(8,128)(2,1)} %copy.83) | copy-start | bytes 12582916
  259.1 10.9 %copy-start.24 = (bf16[1296,1024]{1,0:T(8,128)(2,1)S(1)}, bf16[1296,1024]{1,0:T(8,128)(2,1)}, u32[]{:S(2)}) copy-start(bf16[1296,1024]{1,0:T(8,128)(2,1)} %reshape.216) | copy-start | bytes 7962628
  270.0 8.7 %copy-start.15 = (bf16[128,8,4,512]{3,1,2,0:T(8,128)(2,1)S(1)}, bf16[128,8,4,512]{3,1,2,0:T(8,128)(2,1)}, u32[]{:S(2)}) copy-start(bf16[128,8,4,512]{3,1,2,0:T(8,128)(2,1)} %copy.84) | copy-start | bytes 12582916
  270.0 8.7 %copy-start.25 = (bf16[1296,1024]{1,0:T(8,128)(2,1)S(1)}, bf16[1296,1024]{1,0:T(8,128)(2,1)}, u32[]{:S(2)}) copy-start(bf16[1296,1024]{1,0:T(8,128)(2,1)} %reshape.217) | copy-start | bytes 7962628
  278.7 8.3 %copy-start.14 = (bf16[128,8,4,512]{3,1,2,0:T(8,128)(2,1)S(1)}, bf16[128,8,4,512]{3,1,2,0:T(8,128)(2,1)}, u32[]{:S(2)}) copy-start(bf16[128,8,4,512]{3,1,2,0:T(8,128)(2,1)} %copy.86) | copy-start | bytes 12582916
  278.7 8.3 %copy-start.26 = (bf16[1296,1024]{1,0:T(8,128)(2,1)S(1)}, bf16[1296,1024]{1,0:T(8,128)(2,1)}, u32[]{:S(2)}) copy-start(bf16[1296,1024]{1,0:T(8,128)(2,1)} %reshape.219) | copy-start | bytes 7962628
  287.0 8.2 %copy-start.13 = (bf16[128,8,4,512]{3,1,2,0:T(8,128)(2,1)S(1)}, bf16[128,8,4,512]{3,1,2,0:T(8,128)(2,1)}, u32[]{:S(2)}) copy-start(bf16[128,8,4,512]{3,1,2,0:T(8,128)(2,1)} %copy.87) | copy-start | bytes 12582916
  287.0 8.2 %copy-start.27 = (bf16[1296,1024]{1,0:T(8,128)(2,1)S(1)}, bf16[1296,1024]{1,0:T(8,128)(2,1)}, u32[]{:S(2)}) copy-start(bf16[1296,1024]{1,0:T(8,128)(2,1)} %reshape.220) | copy-start | bytes 7962628
  295.2 8.3 %copy-start = (bf16[128,8,4,512]{3,1,2,0:T(8,128)(2,1)S(1)}, bf16[128,8,4,512]{3,1,2,0:T(8,128)(2,1)}, u32[]{:S(2)}) copy-start(bf16[128,8,4,512]{3,1,2,0:T(8,128)(2,1)} %copy.89) | copy-start | bytes 12582916
  295.2 8.3 %copy-start.51 = (f32[1,4,4,128]{3,1,2,0:T(4,128)S(1)}, f32[1,4,4,128]{3,1,2,0:T(4,128)}, u32[]{:S(2)}) copy-start(f32[1,4,4,128]{3,1,2,0:T(4,128)} %copy.71) | copy-start | bytes 24580
  378.0 24.4 %copy-start.23 = (f32[36,36,512]{2,1,0:T(8,128)S(1)}, f32[36,36,512]{2,1,0:T(8,128)}, u32[]{:S(2)}) copy-start(f32[36,36,512]{2,1,0:T(8,128)} %param.11) | copy-start | bytes 7962628
  402.4 4.5 copy-start.40
  402.4 4.5 copy-start.42
  406.9 5.6 copy-start.48
  406.9 5.7 copy-start.45
  406.9 5.8 copy-start.47
  407.0 6.0 copy-start.44
  407.0 6.1 copy-start.46
  407.0 6.2 copy-start.38
  413.2 5.6 copy-start.36
  418.8 5.6 copy-start.34
  424.4 5.4 copy-start.32
  429.8 5.6 copy-start.30
  455.6 17.6 %collective-permute-start.8 = (bf16[1,36,1024]{2,1,0:T(8,128)(2,1)S(1)}, bf16[1,36,1024]{2,1,0:T(8,128)(2,1)S(1)}, u32[]{:S(2)}, u32[]{:S(2)}) collective-permute-start(bf16[1,36,1024]{2,1,0:T(8,128)(2,1)S(1)} %get-tuple-element.49), channel_id=1, source_target_pairs={{0,8},{8,16},{16,24},{1,9},{9,17},{17,25},{2,10},{10,18},{18,26},{... | collective-permute-start | bytes 221192 | tf_op jit(solution)/shard_map/ppermute | solution.py:17
  457.4 15.8 %collective-permute-start.9 = (bf16[1,36,1024]{2,1,0:T(8,128)(2,1)S(1)}, bf16[1,36,1024]{2,1,0:T(8,128)(2,1)S(1)}, u32[]{:S(2)}, u32[]{:S(2)}) collective-permute-start(bf16[1,36,1024]{2,1,0:T(8,128)(2,1)S(1)} %get-tuple-element.48), channel_id=1, source_target_pairs={{8,0},{16,8},{24,16},{9,1},{17,9},{25,17},{10,2},{18,10},{26,18},{... | collective-permute-start | bytes 221192 | tf_op jit(solution)/shard_map/ppermute | solution.py:19
  462.6 10.6 %copy-start.11 = (bf16[36,36,1024]{2,1,0:T(8,128)(2,1)S(1)}, bf16[36,36,1024]{2,1,0:T(8,128)(2,1)}, u32[]{:S(2)}) copy-start(bf16[36,36,1024]{2,1,0:T(8,128)(2,1)} %all-gather.5.cloned.1.call-done) | copy-start | bytes 7962628
  478.4 33.2 %collective-permute-start.10 = (bf16[38,1,1024]{2,1,0:T(2,128)(2,1)}, bf16[38,1,1024]{2,1,0:T(2,128)(2,1)S(1)}, u32[]{:S(2)}, u32[]{:S(2)}) collective-permute-start(bf16[38,1,1024]{2,1,0:T(2,128)(2,1)} %get-tuple-element.38), channel_id=1, source_target_pairs={{0,2},{2,4},{4,6},{1,3},{3,5},{5,7},{8,10},{10,12},{12,14},{9,11},... | collective-permute-start | bytes 233480 | tf_op jit(solution)/shard_map/ppermute | solution.py:17
  481.8 29.8 %collective-permute-start.11 = (bf16[38,1,1024]{2,1,0:T(2,128)(2,1)S(1)}, bf16[38,1,1024]{2,1,0:T(2,128)(2,1)S(1)}, u32[]{:S(2)}, u32[]{:S(2)}) collective-permute-start(bf16[38,1,1024]{2,1,0:T(2,128)(2,1)S(1)} %get-tuple-element.39), channel_id=1, source_target_pairs={{2,0},{4,2},{6,4},{3,1},{5,3},{7,5},{10,8},{12,10},{14,12},{11,9},... | collective-permute-start | bytes 233480 | tf_op jit(solution)/shard_map/ppermute | solution.py:19
  500.9 10.8 %copy-start.21 = (bf16[38,36,1024]{2,1,0:T(8,128)(2,1)S(1)}, bf16[38,36,1024]{2,1,0:T(8,128)(2,1)}, u32[]{:S(2)}) copy-start(bf16[38,36,1024]{2,1,0:T(8,128)(2,1)} %copy-done.20) | copy-start | bytes 8404996
  596.3 3.5 copy-start.52
  673.2 24.4 %copy-start.12 = (f32[36,36,512]{2,1,0:T(8,128)S(1)}, f32[36,36,512]{2,1,0:T(8,128)}, u32[]{:S(2)}) copy-start(f32[36,36,512]{2,1,0:T(8,128)} %get-tuple-element.5) | copy-start | bytes 7962628
  (4 other events, 9.9 us)
Sparse Core Ops, SparseCore 0:
  9.5 45.4 all-gather.2
  407.0 47.6 all-gather.4
where the time goes:
time: 718 us; the launch traced here: 709 us
  matrix products  379 us (53%)
  local copies, waits for them, and re-layouts  234 us (33%)
  other arithmetic  37.1 us (5%)
  starting transfers between devices  28.7 us (4%)
  between operations  15.1 us (2%)
  waiting for transfers between devices  14.7 us (2%)
    dot_general x36, matrix products, taps_sum(): jnp.dot(window, kernels[tap], preferred_element_type=jnp.float32)  379 us
    reshape x36, local copies, waits for them, and re-layouts, taps_sum(): window = window.reshape(rows * cols, window.shape[2])  85.4 us
    slice x2, local copies, waits for them, and re-layouts, per_device(): gates[:, :, 1]  48.8 us
    unnamed x130, local copies, waits for them, and re-layouts  35 us
    slice x2, local copies, waits for them, and re-layouts, taps_sum(): kernels[tap]  29.2 us
    concatenate x6, other arithmetic, with_halo(): jnp.concatenate([lax.ppermute(tail, axis, [(i, (i + 1) % count) for i in...  28.2 us
    reshape x2, local copies, waits for them, and re-layouts, per_device(): gates = total.reshape(rows, cols, 4, width)  27.1 us
    ppermute x6, starting transfers between devices, with_halo(): lax.ppermute(tail, axis, [(i, (i + 1) % count) for i in range(ends)])  20.7 us
  transfers between devices with their start and end apart: 14, of which 1 were waited for; matrix products, arithmetic and copies ran while one was open for 37% of the time, Pallas kernels for 0%

commit v1 on v0

v1 whole, which is shorter than its diff:
```python
import functools

import jax
import jax.numpy as jnp
from jax import lax
from jax.experimental import pallas as pl
from jax.experimental.pallas import tpu as pltpu
from jax.sharding import PartitionSpec as P

STEPS = 2
LANES = 128
F32 = jnp.float32
BF16 = jnp.bfloat16
VMEM = 60 * 2**20


def up_to(value, multiple):
    return -(-value // multiple) * multiple


def weights_kernel(depth, blocks, w_ref, u_ref, wide_ref):
    for j in range(blocks):
        lanes = slice(LANES * j, LANES * j + LANES)
        for a in range(3):
            wide_ref[a] = w_ref[a, 0, :, :, lanes].astype(F32).reshape(depth * 4, LANES)
        for gate in range(4):
            g0, g1, g2 = [wide_ref[a, pl.ds(gate, depth, stride=4), :] for a in range(3)]
            ends = g0 + g2
            out = slice(LANES * gate, LANES * gate + LANES)
            u_ref[j, 0, 0, :, out] = (ends + g1).astype(BF16)
            u_ref[j, 0, 1, :, out] = (ends - g1).astype(BF16)
            u_ref[j, 1, 0, :, out] = g0.astype(BF16)
            u_ref[j, 1, 1, :, out] = g2.astype(BF16)


def transformed_weights(w_hidden):
    channels, width = w_hidden.shape[1], w_hidden.shape[3]
    blocks = width // LANES
    depth = 256
    steps = channels // depth
    w = w_hidden.reshape(3, 3, channels, 4, width)
    return pl.pallas_call(
        functools.partial(weights_kernel, depth, blocks),
        grid=(3, steps),
        in_specs=[pl.BlockSpec((3, 1, depth, 4, width), lambda b, k: (0, b, k, 0, 0))],
        out_specs=pl.BlockSpec(
            (blocks, 2, 2, depth, 4 * LANES), lambda b, k: (0, 0, 0, b * steps + k, 0)
        ),
        out_shape=jax.ShapeDtypeStruct((blocks, 2, 2, 3 * channels, 4 * LANES), BF16),
        scratch_shapes=[pltpu.VMEM((3, depth * 4, LANES), F32)],
        compiler_params=pltpu.CompilerParams(vmem_limit_bytes=VMEM),
        cost_estimate=pl.CostEstimate(
            flops=0, bytes_accessed=42 * channels * 4 * width, transcendentals=0
        ),
        name="weights",
    )(w)


def sigmoid(x):
    return 0.5 * jnp.tanh(0.5 * x) + 0.5


def step_kernel(dims, offset_ref, *refs):
    stride, height, tiles, parts, last, cols = dims
    hidden_refs, refs = refs[:parts], refs[parts:]
    frame_ref, u_ref, w_ref, bias_ref, cell_ref = refs[:5]
    refs = refs[5:]
    if not last:
        mask_ref, refs = refs[0], refs[1:]
    hidden_out, cell_out, v_ref, x_ref, pre_ref, wide_ref = refs
    channels = v_ref.shape[2] // 3
    half = pl.program_id(1)

    @pl.when((pl.program_id(0) == 0) & (half == 0))
    def _():
        fill = wide_ref.shape[1] - frame_ref.shape[1]
        wide_ref[:, frame_ref.shape[1] :, :] = jnp.zeros((2, fill, LANES), F32)
        wide_ref[:, : frame_ref.shape[1], :] = frame_ref[...].astype(F32)
        for p in range(2):
            for a in range(3):
                for one in range(2):
                    start = stride * ((p + a) // 2) + one
                    at = 256 * a + LANES * one
                    x_ref[p, :, at : at + LANES] = wide_ref[
                        (p + a) % 2, start : start + height, :
                    ].astype(BF16)
        for part, hidden_ref in enumerate(hidden_refs):
            rows = hidden_ref.shape[1]

            @pl.loop(0, hidden_ref.shape[2] // LANES)
            def _(j):
                at = pl.multiple_of(j * LANES, LANES)
                wide_ref[:, :rows, :] = hidden_ref[:, :, pl.ds(at, LANES)].astype(F32)
                for b in range(3):
                    d0 = wide_ref[0, b : b + height, :]
                    d1 = wide_ref[1, b : b + height, :]
                    d2 = wide_ref[0, stride + b : stride + b + height, :]
                    d3 = wide_ref[1, stride + b : stride + b + height, :]
                    to = pl.multiple_of(offset_ref[part] + j * LANES + b * channels, LANES)
                    v_ref[0, :, pl.ds(to, LANES)] = (d0 - d2).astype(BF16)
                    v_ref[1, :, pl.ds(to, LANES)] = (d1 + d2).astype(BF16)
                    v_ref[2, :, pl.ds(to, LANES)] = (d2 - d1).astype(BF16)
                    v_ref[3, :, pl.ds(to, LANES)] = (d1 - d3).astype(BF16)

    def dot(a, b):
        return jnp.dot(a, b, preferred_element_type=F32)

    @pl.when(half == 0)
    def _():
        for low, high in tiles:
            m = slice(low, high)
            plus = dot(v_ref[1, m, :], u_ref[0, 0, 0])
            minus = dot(v_ref[2, m, :], u_ref[0, 0, 1])
            pre_ref[0, m, :] = 0.5 * (plus + minus) + (dot(x_ref[0, m, :], w_ref[0]) + bias_ref[0])
            pre_ref[1, m, :] = 0.5 * (plus - minus) + (dot(x_ref[1, m, :], w_ref[0]) + bias_ref[0])

    @pl.when(half == 1)
    def _():
        for low, high in tiles:
            m = slice(low, high)
            for p in range(2):
                edge = dot(v_ref[3 * p, m, :], u_ref[0, 0, p])
                pre = pre_ref[p, m, :] - edge if p else pre_ref[p, m, :] + edge
                i, f, o, g = [pre[:, LANES * k : LANES * k + LANES] for k in range(4)]
                if last:
                    skip = 1 + stride * p
                    before = cell_ref[0, 1 - p, low + skip : high + skip, :]
                else:
                    before = cell_ref[p, m, :]
                cell = sigmoid(f) * before + sigmoid(i) * jnp.tanh(g)
                hidden = sigmoid(o) * jnp.tanh(cell)
                if last:
                    for t in range(low // stride, high // stride):
                        r = slice(t * stride - low, t * stride - low + cols)
                        cell_out[2 * t + p] = cell[r]
                        hidden_out[2 * t + p] = hidden[r].astype(BF16)
                else:
                    cell_out[0, p, m, :] = cell
                    hidden_out[p, m, :] = jnp.where(mask_ref[p, m, :] > 0, hidden, 0).astype(BF16)


def run_step(offsets, hiddens, frame, u, w_in, bias, cell, mask, stride, pairs, rows, cols):
    last = mask is None
    blocks = u.shape[0]
    channels = u.shape[3] // 3
    height = up_to(pairs * stride, 16)
    cut = stride * 2
    middle = up_to(height // 2, cut) if last else height // 2
    tiles = ((0, middle), (middle, height))
    parts = len(hiddens)
    wide = up_to(max(h.shape[1] for h in hiddens + [frame]), 8)
    wide = up_to(max(wide, height + stride + 2), 8)
    dims = (stride, height, tiles, parts, last, cols)
    once = pl.Buffered(1)
    whole = lambda array: pl.BlockSpec(
        array.shape, lambda n, s: (0,) * array.ndim, pipeline_mode=once
    )
    in_specs = [pl.BlockSpec(memory_space=pltpu.SMEM)]
    in_specs += [whole(h) for h in hiddens]
    in_specs += [
        whole(frame),
        pl.BlockSpec((1, 1, 2, 3 * channels, 4 * LANES), lambda n, s: (n, s, 0, 0, 0)),
        pl.BlockSpec((1, w_in.shape[1], 4 * LANES), lambda n, s: (n, 0, 0)),
        pl.BlockSpec((1, 1, 4 * LANES), lambda n, s: (n, 0, 0)),
    ]
    args = [offsets, *hiddens, frame, u, w_in, bias, cell]
    if last:
        in_specs.append(pl.BlockSpec((1,) + cell.shape[1:], lambda n, s: (n, 0, 0, 0)))
        shape = (rows, cols, blocks * LANES)
        out_specs = (pl.BlockSpec((rows, cols, LANES), lambda n, s: (0, 0, n)),) * 2
        out_shape = (jax.ShapeDtypeStruct(shape, BF16), jax.ShapeDtypeStruct(shape, F32))
    else:
        in_specs.append(pl.BlockSpec((2, height, LANES), lambda n, s: (0, 0, n)))
        in_specs.append(whole(mask))
        args.append(mask)
        out_specs = (
            pl.BlockSpec((2, height, LANES), lambda n, s: (0, 0, n)),
            pl.BlockSpec((1, 2, height, LANES), lambda n, s: (n, 0, 0, 0)),
        )
        out_shape = (
            jax.ShapeDtypeStruct((2, height, blocks * LANES), BF16),
            jax.ShapeDtypeStruct((blocks, 2, height, LANES), F32),
        )
    flops = 2 * height * blocks * 4 * LANES * (12 * channels + 2 * w_in.shape[1])
    return pl.pallas_call(
        functools.partial(step_kernel, dims),
        grid=(blocks, 2),
        in_specs=in_specs,
        out_specs=out_specs,
        out_shape=out_shape,
        scratch_shapes=[
            pltpu.VMEM((4, height, 3 * channels), BF16),
            pltpu.VMEM((2, height, w_in.shape[1]), BF16),
            pltpu.VMEM((2, height, 4 * LANES), F32),
            pltpu.VMEM((2, wide, LANES), F32),
        ],
        compiler_params=pltpu.CompilerParams(vmem_limit_bytes=VMEM),
        cost_estimate=pl.CostEstimate(
            flops=flops, bytes_accessed=u.size * 2, transcendentals=height * blocks * LANES * 10
        ),
        name="step",
    )(*args)


def forward(x, axis):
    count = lax.axis_size(axis)
    return lax.ppermute(x, axis, [(i, i + 1) for i in range(count - 1)])


def backward(x, axis):
    count = lax.axis_size(axis)
    return lax.ppermute(x, axis, [(i + 1, i) for i in range(count - 1)])


def split(x):
    high = lax.reduce_precision(x, 8, 7)
    return high.astype(BF16), (x - high).astype(BF16)


def joined(high, low):
    return high.astype(F32) + low.astype(F32)


def extended(hidden, frames, cell, axis, dim):
    size = hidden.shape[dim]

    def packed(two, one):
        high, low = split(lax.slice_in_dim(cell, one, one + 1, axis=dim))
        ends = jnp.concatenate([high, low], axis=dim)
        taken = [lax.slice_in_dim(a, two, two + 2, axis=dim) for a in (hidden, frames)]
        if dim == 1:
            extra = hidden.shape[0] - cell.shape[0]
            ends = jnp.pad(ends, ((0, extra), (0, 0), (0, 0)))
        return jnp.concatenate(taken + [ends], axis=2)

    before = forward(packed(size - 2, cell.shape[dim] - 1), axis)
    after = backward(packed(0, 0), axis)
    first, second = hidden.shape[2], hidden.shape[2] + frames.shape[2]

    def one(got):
        ends = got[: cell.shape[0], :, second:] if dim == 1 else got[:, :, second:]
        high = lax.slice_in_dim(ends, 0, 1, axis=dim)
        low = lax.slice_in_dim(ends, 1, 2, axis=dim)
        return joined(high, low)

    return (
        jnp.concatenate([before[:, :, :first], hidden, after[:, :, :first]], axis=dim),
        jnp.concatenate(
            [before[:, :, first:second], frames, after[:, :, first:second]], axis=dim
        ),
        jnp.concatenate([one(before), cell, one(after)], axis=dim),
    )


def planes(x, stride):
    rows, cols, channels = x.shape
    x = jnp.pad(x, ((0, 0), (0, stride - cols), (0, 0)))
    x = x.reshape(rows // 2, 2, stride, channels).transpose(1, 0, 2, 3)
    return x.reshape(2, rows // 2 * stride, channels)


def frame_planes(frame, stride):
    beside = jnp.pad(frame[:, 1:], ((0, 0), (0, 1), (0, 0)))
    return planes(jnp.concatenate([frame, beside], axis=2), stride)


def gathered(hidden):
    count = lax.axis_size("ch")
    width = hidden.shape[2]
    if count == 2:
        other = lax.ppermute(hidden, "ch", [(0, 1), (1, 0)])
        me = lax.axis_index("ch")
        return [hidden, other], jnp.stack([me * width, (1 - me) * width]).astype(jnp.int32)
    every = lax.all_gather(hidden, "ch")
    return [every[i] for i in range(count)], jnp.arange(count, dtype=jnp.int32) * width


def input_weights(w_input):
    _, depth, _, width = w_input.shape
    w = w_input.reshape(3, 3, depth, 4, width // LANES, LANES)
    w = jnp.stack([w[:, 0], w[:, 1], jnp.zeros_like(w[:, 1]), w[:, 2]], axis=1)
    return w.transpose(4, 0, 1, 2, 3, 5).reshape(width // LANES, 12 * depth, 4 * LANES)


def inside(rows, cols, stride, height):
    p = lax.broadcasted_iota(jnp.int32, (2, height, LANES), 0)
    flat = lax.broadcasted_iota(jnp.int32, (2, height, LANES), 1)
    y = 2 * (flat // stride) + p - 1 + lax.axis_index("sy") * rows
    x = flat % stride - 1
    wholly = (x <= cols) & (flat // stride <= rows // 2)
    x = x + lax.axis_index("sx") * cols
    ny, nx = rows * lax.axis_size("sy"), cols * lax.axis_size("sx")
    return ((y >= 0) & (y < ny) & (x >= 0) & (x < nx) & wholly).astype(F32)


def per_device(frames, w_input, w_hidden, biases, hidden_init, cell_init):
    rows, cols, width = hidden_init.shape
    stride = up_to(cols + 4, 8)
    half = frames.shape[2] // STEPS
    blocks = width // LANES
    u = transformed_weights(w_hidden)
    w_in = input_weights(w_input)
    bias = biases.reshape(4, blocks, LANES).transpose(1, 0, 2).reshape(blocks, 1, 4 * LANES)
    wider = extended(hidden_init, frames, cell_init, "sy", 0)
    hidden, framed, cell = extended(*wider, "sx", 1)
    hiddens, offsets = gathered(planes(hidden, stride))
    height = up_to((rows // 2 + 1) * stride, 16)
    cell = planes(cell, stride)
    cell = jnp.pad(cell, ((0, 0), (0, height - cell.shape[1]), (0, 0)))
    mask = inside(rows, cols, stride, height)
    frame = frame_planes(framed[:, :, :half], stride)
    hidden, cell = run_step(
        offsets, hiddens, frame, u, w_in, bias, cell, mask, stride, rows // 2 + 1, rows, cols
    )
    hiddens, offsets = gathered(hidden)
    frame = frame_planes(framed[1:-1, 1:-1, half:], stride)
    return run_step(
        offsets, hiddens, frame, u, w_in, bias, cell, None, stride, rows // 2, rows, cols
    )


def solution(mesh):
    in_specs = (
        P("sy", "sx", None),
        P(None, None, None, "ch"),
        P(None, None, None, "ch"),
        P(None, "ch"),
        P("sy", "sx", "ch"),
        P("sy", "sx", "ch"),
    )
    out_specs = (P("sy", "sx", "ch"), P("sy", "sx", "ch"))
    return jax.shard_map(
        per_device, mesh=mesh, in_specs=in_specs, out_specs=out_specs, check_vma=False
    )
```

time: 718 us -> 284 us (0.40); the launches traced: 709 us -> 283 us
  matrix products: 379 us -> 0 us
  local copies, waits for them, and re-layouts: 234 us -> 27 us
  Pallas kernels: 0 us -> 158 us
  waiting for transfers between devices: 14.7 us -> 67.1 us
  other arithmetic: 37.1 us -> 14.5 us
  starting transfers between devices: 28.7 us -> 14.5 us
  between operations: 15.1 us -> 1.09 us
    dot_general x36 -> x0, matrix products: 379 us -> none  [taps_sum(): jnp.dot(window, kernels[tap], preferred_element_type=jnp.float32)]
    pallas_call x0 -> x3, Pallas kernels: none -> 158 us  [the longest x2 118 us: run_step(): pl.pallas_call(functools.partial(step_kernel, dims), grid=(blocks, 2), in...]
    reshape x38 -> x5, local copies, waits for them, and re-layouts: 112 us -> 14.5 us  [the longest x1 5.72 us: input_weights(): w.transpose(4, 0, 1, 2, 3, 5).reshape(width // LANES, 12 * depth, 4 * LANES)]
    slice x15 -> x22, local copies, waits for them, and re-layouts: 86.3 us -> 4.66 us  [the longest x4 1.71 us: packed(): lax.slice_in_dim(a, two, two + 2, axis=dim)]
    ppermute x12 -> x6, waiting for transfers between devices: 0.03 us -> 67.1 us  [the longest x2 62.2 us: gathered(): other = lax.ppermute(hidden, 'ch', [(0, 1), (1, 0)])]
    unnamed x130 -> x35, local copies, waits for them, and re-layouts: 35 us -> 4.62 us
    concatenate x6 -> x11, other arithmetic: 28.2 us -> 3.98 us  [the longest x3 1.46 us: packed(): return jnp.concatenate(taken + [ends], axis=2)]
    ppermute x12 -> x6, starting transfers between devices: 28.6 us -> 14.5 us  [the longest x2 8.64 us: forward(): return lax.ppermute(x, axis, [(i, i + 1) for i in range(count - 1)])]
  transfers between devices with their start and end apart: 14 -> 6, of which waited for: 1 -> 4; matrix products, arithmetic and copies ran while one was open for 37% -> 9% of each run, Pallas kernels for 0% -> 14%
where the time goes in v1:
time: 284 us; the launch traced here: 283 us
  Pallas kernels  158 us (56%)
  waiting for transfers between devices  67.1 us (24%)
  local copies, waits for them, and re-layouts  27 us (10%)
  other arithmetic  14.5 us (5%)
  starting transfers between devices  14.5 us (5%)
    pallas_call x2, Pallas kernels, run_step(): pl.pallas_call(functools.partial(step_kernel, dims), grid=(blocks, 2), in...  118 us
    ppermute x2, waiting for transfers between devices, gathered(): other = lax.ppermute(hidden, 'ch', [(0, 1), (1, 0)])  62.2 us
    pallas_call x1, Pallas kernels, transformed_weights(): pl.pallas_call(functools.partial(weights_kernel, depth, blocks), grid=(3,...  40.5 us
    ppermute x2, starting transfers between devices, forward(): return lax.ppermute(x, axis, [(i, i + 1) for i in range(count - 1)])  8.64 us
    reshape x1, local copies, waits for them, and re-layouts, input_weights(): w.transpose(4, 0, 1, 2, 3, 5).reshape(width // LANES, 12 * depth, 4 * LANES)  5.72 us
  transfers between devices with their start and end apart: 6, of which 4 were waited for; matrix products, arithmetic and copies ran while one was open for 9% of the time, Pallas kernels for 14%

profile of v1, /device:TPU:0, one launch (start us, length us, event | category | flops | bytes accessed | tf_op | source)
XLA Modules:
  0.0 282.7 jit_solution(17045208246480850474)
XLA Ops:
  0.6 0.8 fusion.55
  1.4 0.9 reduce-precision_convert_fusion.1
  2.3 0.9 fusion.54
  3.3 0.7 maximum_maximum_fusion.1
  4.0 1.3 collective-permute-start.1
  5.3 0.7 maximum_maximum_fusion
  6.0 3.7 %collective-permute-start = (bf16[2,36,1152]{2,1,0:T(8,128)(2,1)}, bf16[2,36,1152]{2,1,0:T(8,128)(2,1)}, u32[]{:S(2)}, u32[]{:S(2)}) collective-permute-start(bf16[2,36,1152]{2,1,0:T(8,128)(2,1)} %maximum_maximum_fusion), channel_id=1, source_target_pairs={{0,8},{8,16},{16,24},{1,9},{9,17},{17,25},{2,10},{10,18},{18,26},{... | collective-permute-start | bytes 497672 | tf_op jit(solution)/shard_map/ppermute | solution.py:207
  9.7 4.3 %reshape.48 = bf16[3,3,64,4,4,128]{5,4,3,2,1,0:T(4,128)(2,1)S(1)} reshape(bf16[9,64,4,512]{3,2,1,0:T(4,128)(2,1)} %param.7) | data formatting | bytes 4718592 | tf_op jit(solution)/shard_map/reshape | solution.py:280
  14.0 0.3 slice.168
  14.3 0.5 slice.167
  14.9 0.8 copy.55
  15.7 0.3 copy.56
  16.0 0.0 copy-start.2
  16.0 0.1 pad.46.clone
  16.1 3.5 %maximum_bitcast_fusion = bf16[4,3,4,64,4,128]{5,4,3,2,1,0:T(4,128)(2,1)} fusion(bf16[3,1,64,4,4,128]{5,3,2,1,0,4:T(4,128)(2,1)S(1)} %copy.56, bf16[3,2,64,4,4,128]{5,3,2,1,0,4:T(4,128)(2,1)S(1)} %copy.55, bf16[4]{0:T(256)(128)(2,1)S(1)} %pad.46.clone), kind=kLoop, calls=%fused_computation | loop fusion | flops 3145728 | bytes 5505032 | tf_op jit(solution)/shard_map/transpose | solution.py:282
  19.6 0.6 fusion.51
  20.2 0.4 copy.32
  20.6 5.7 %reshape.49.refs_4_ = bf16[4,768,512]{2,1,0:T(8,128)(2,1)} reshape(bf16[4,3,4,64,4,128]{5,4,3,2,1,0:T(4,128)(2,1)} %maximum_bitcast_fusion) | data formatting | bytes 6291456 | tf_op jit(solution)/shard_map/reshape | solution.py:282
  26.4 40.5 %weights.1.refs_3_ = bf16[4,2,2,3072,512]{4,3,2,1,0:T(8,128)(2,1)} custom-call(bf16[3,3,1024,4,512]{4,3,2,1,0:T(4,128)(2,1)} %bitcast.29), custom_call_target="tpu_custom_call" | custom-call | bytes 88080384 | tf_op jit(solution)/shard_map/weights/pallas_call | solution.py:42
  66.9 0.0 collective-permute-done.1
  66.9 0.1 copy.33
  67.0 0.0 collective-permute-done
  67.0 0.7 slice.155
  67.8 0.9 slice.153
  68.7 0.1 copy.31
  68.8 0.8 convert_add_fusion.1
  69.6 0.0 copy-start.6
  69.6 1.5 reduce-precision_convert_fusion.3
  71.1 0.1 fusion.44
  71.4 0.1 fusion.35
  71.5 4.9 %collective-permute-start.2 = (bf16[40,2,1152]{2,0,1:T(8,128)(2,1)S(1)}, bf16[40,2,1152]{2,0,1:T(8,128)(2,1)S(1)}, u32[]{:S(2)}, u32[]{:S(2)}) collective-permute-start(bf16[40,2,1152]{2,0,1:T(8,128)(2,1)S(1)} %get-tuple-element.16), channel_id=1, source_target_pairs={{0,2},{2,4},{4,6},{1,3},{3,5},{5,7},{8,10},{10,12},{12,14},{9,11},... | collective-permute-start | bytes 552968 | tf_op jit(solution)/shard_map/ppermute | solution.py:207
  76.4 1.5 collective-permute-start.3
  77.9 2.2 fusion.19.refs_7_
  80.1 0.8 collective-permute-done.2
  80.9 4.1 %collective-permute-done.3 = bf16[40,2,1152]{2,0,1:T(8,128)(2,1)S(1)} collective-permute-done((bf16[40,2,1152]{2,0,1:T(8,128)(2,1)S(1)}, bf16[40,2,1152]{2,0,1:T(8,128)(2,1)S(1)}, u32[]{:S(2)}, u32[]{:S(2)}) %collective-permute-start.3) | collective-permute-done | bytes 184352 | tf_op jit(solution)/shard_map/ppermute | solution.py:212
  85.0 0.7 copy-done.10
  85.7 1.0 pad_maximum_fusion
  86.7 0.0 slice-start
  86.7 0.0 slice-start.1
  86.7 1.5 reshape.43
  88.3 2.1 copy.40
  90.4 0.0 copy-start.3
  90.4 1.6 collective-permute-start.4
  92.0 0.6 pad_add_fusion.offset_ref
  92.6 0.2 pad_maximum_fusion.1
  92.8 0.1 slice.166
  93.0 0.3 fusion.27
  93.2 0.8 copy.43
  94.1 0.1 fusion.47
  94.1 0.1 fusion.46
  94.3 0.6 select_maximum_fusion
  94.9 0.4 copy.51
  95.3 2.0 pad.31.refs_6_
  97.2 30.2 %collective-permute-done.4.refs_1_ = bf16[2,800,512]{2,1,0:T(8,128)(2,1)S(1)} collective-permute-done((bf16[2,800,512]{2,1,0:T(8,128)(2,1)S(1)}, bf16[2,800,512]{2,1,0:T(8,128)(2,1)S(1)}, u32[]{:S(2)}, u32[]{:S(2)}) %collective-permute-start.4) | collective-permute-done | bytes 1638432 | tf_op jit(solution)/shard_map/ppermute | solution.py:271
  127.5 1.1 copy-done.13
  128.6 60.9 %step.2 = (bf16[2,768,512]{2,1,0:T(8,128)(2,1)}, f32[4,2,768,128]{3,2,1,0:T(8,128)}) custom-call(s32[2]{0:T(128)} %pad_add_fusion.offset_ref, bf16[2,800,512]{2,1,0:T(8,128)(2,1)} %bitcast.34, bf16[2,800,512]{2,1,0:T(8,128)(2,1)} %copy-done.13, bf16[2,800,128]{2,1,0:T(8,128)(2,1)} %bitcast.37, bf16[4,2,2,3072,512]{4,3,2,1,0:T(8,128)(2,1)} %weights.1.refs_3_, ...), custom_call_target="tpu_custom_call" | custom-call | flops 43486543872 | bytes 50331648 | tf_op jit(solution)/shard_map/step/pallas_call | solution.py:185
  189.5 1.5 collective-permute-start.5
  191.0 0.2 slice.173
  191.3 0.2 fusion.30
  191.5 0.2 fusion.31
  191.7 0.8 copy.52
  192.5 31.9 %collective-permute-done.5.refs_1_ = bf16[2,768,512]{2,1,0:T(8,128)(2,1)S(1)} collective-permute-done((bf16[2,768,512]{2,1,0:T(8,128)(2,1)}, bf16[2,768,512]{2,1,0:T(8,128)(2,1)S(1)}, u32[]{:S(2)}, u32[]{:S(2)}) %collective-permute-start.5) | collective-permute-done | bytes 1572896 | tf_op jit(solution)/shard_map/ppermute | solution.py:271
  224.4 1.1 copy-done.14
  225.6 57.1 %step.3 = (bf16[36,36,512]{2,1,0:T(8,128)(2,1)}, f32[36,36,512]{2,1,0:T(8,128)}) custom-call(s32[2]{0:T(128)} %pad_add_fusion.offset_ref, bf16[2,768,512]{2,1,0:T(8,128)(2,1)} %get-tuple-element.4.refs_0_, bf16[2,768,512]{2,1,0:T(8,128)(2,1)} %copy-done.14, bf16[2,760,128]{2,1,0:T(8,128)(2,1)} %bitcast.38, bf16[4,2,2,3072,512]{4,3,2,1,0:T(8,128)(2,1)} %weights.1.refs_3_, ...), custom_call_target="tpu_custom_call" | custom-call | flops 40768634880 | bytes 50331648 | tf_op jit(solution)/shard_map/step/pallas_call | solution.py:185
  (46 shorter events, 0.3 us)
Async XLA Ops:
  4.0 62.9 %collective-permute-start.1 = (bf16[2,36,1152]{2,1,0:T(8,128)(2,1)}, bf16[2,36,1152]{2,1,0:T(8,128)(2,1)S(1)}, u32[]{:S(2)}, u32[]{:S(2)}) collective-permute-start(bf16[2,36,1152]{2,1,0:T(8,128)(2,1)} %maximum_maximum_fusion.1), channel_id=1, source_target_pairs={{8,0},{16,8},{24,16},{9,1},{17,9},{25,17},{10,2},{18,10},{26,18},{... | collective-permute-start | bytes 497672 | tf_op jit(solution)/shard_map/ppermute | solution.py:212
  6.0 61.0 %collective-permute-start = (bf16[2,36,1152]{2,1,0:T(8,128)(2,1)}, bf16[2,36,1152]{2,1,0:T(8,128)(2,1)}, u32[]{:S(2)}, u32[]{:S(2)}) collective-permute-start(bf16[2,36,1152]{2,1,0:T(8,128)(2,1)} %maximum_maximum_fusion), channel_id=1, source_target_pairs={{0,8},{8,16},{16,24},{1,9},{9,17},{17,25},{2,10},{10,18},{18,26},{... | collective-permute-start | bytes 497672 | tf_op jit(solution)/shard_map/ppermute | solution.py:207
  16.0 4.2 %copy-start.2 = (bf16[36,36,512]{2,1,0:T(8,128)(2,1)S(1)}, bf16[36,36,512]{2,1,0:T(8,128)(2,1)}, u32[]{:S(2)}) copy-start(bf16[36,36,512]{2,1,0:T(8,128)(2,1)} %param.10) | copy-start | bytes 3981316
  26.4 41.4 %copy-start.1 = (bf16[36,36,128]{2,1,0:T(8,128)(2,1)S(1)}, bf16[36,36,128]{2,1,0:T(8,128)(2,1)}, u32[]{:S(2)}) copy-start(bf16[36,36,128]{2,1,0:T(8,128)(2,1)} %param.6) | copy-start | bytes 995332
  68.8 2.7 copy-start.4
  69.6 1.8 copy-start.6
  69.6 8.3 %copy-start.12 = (pred[768]{0:T(1024)(128)(4,1)S(1)}, pred[768]{0:T(1024)(128)(4,1)}, u32[]{:S(2)}) copy-start(pred[768]{0:T(1024)(128)(4,1)} %get-tuple-element.35) | copy-start | bytes 2308
  71.5 9.4 %collective-permute-start.2 = (bf16[40,2,1152]{2,0,1:T(8,128)(2,1)S(1)}, bf16[40,2,1152]{2,0,1:T(8,128)(2,1)S(1)}, u32[]{:S(2)}, u32[]{:S(2)}) collective-permute-start(bf16[40,2,1152]{2,0,1:T(8,128)(2,1)S(1)} %get-tuple-element.16), channel_id=1, source_target_pairs={{0,2},{2,4},{4,6},{1,3},{3,5},{5,7},{8,10},{10,12},{12,14},{9,11},... | collective-permute-start | bytes 552968 | tf_op jit(solution)/shard_map/ppermute | solution.py:207
  76.4 8.6 %collective-permute-start.3 = (bf16[40,2,1152]{2,0,1:T(8,128)(2,1)S(1)}, bf16[40,2,1152]{2,0,1:T(8,128)(2,1)S(1)}, u32[]{:S(2)}, u32[]{:S(2)}) collective-permute-start(bf16[40,2,1152]{2,0,1:T(8,128)(2,1)S(1)} %get-tuple-element.17), channel_id=1, source_target_pairs={{2,0},{4,2},{6,4},{3,1},{5,3},{7,5},{10,8},{12,10},{14,12},{11,9},... | collective-permute-start | bytes 552968 | tf_op jit(solution)/shard_map/ppermute | solution.py:212
  80.9 4.1 %copy-start.8 = (bf16[40,2,1152]{2,0,1:T(8,128)(2,1)}, bf16[40,2,1152]{2,0,1:T(8,128)(2,1)S(1)}, u32[]{:S(2)}) copy-start(bf16[40,2,1152]{2,0,1:T(8,128)(2,1)S(1)} %collective-permute-done.2) | copy-start | bytes 552964
  85.0 0.7 copy-start.10
  86.7 5.9 %slice-start = ((bf16[40,2,1152]{2,0,1:T(8,128)(2,1)}), bf16[40,2,128]{2,0,1:T(8,128)(2,1)S(1)}, s32[]{:S(2)}) async-start(bf16[40,2,1152]{2,0,1:T(8,128)(2,1)} %copy-done.8), calls=%async_computation | async-start | bytes 40960 | tf_op jit(solution)/shard_map/slice | solution.py:249
  86.7 5.9 %slice-start.1 = ((bf16[40,2,1152]{2,0,1:T(8,128)(2,1)}), bf16[40,2,128]{2,0,1:T(8,128)(2,1)S(1)}, s32[]{:S(2)}) async-start(bf16[40,2,1152]{2,0,1:T(8,128)(2,1)} %copy-done.10), calls=%async_computation.1 | async-start | bytes 40960 | tf_op jit(solution)/shard_map/slice | solution.py:249
  88.3 5.8 %copy-start.9 = (bf16[40,2,1152]{2,0,1:T(8,128)(2,1)S(1)}, bf16[40,2,1152]{2,0,1:T(8,128)(2,1)}, u32[]{:S(2)}) copy-start(bf16[40,2,1152]{2,0,1:T(8,128)(2,1)} %copy-done.8) | copy-start | bytes 552964
  88.3 5.8 %copy-start.11 = (bf16[40,2,1152]{2,0,1:T(8,128)(2,1)S(1)}, bf16[40,2,1152]{2,0,1:T(8,128)(2,1)}, u32[]{:S(2)}) copy-start(bf16[40,2,1152]{2,0,1:T(8,128)(2,1)} %copy-done.10) | copy-start | bytes 552964
  88.3 6.0 %copy-start = (f32[36,36,512]{2,1,0:T(8,128)S(1)}, f32[36,36,512]{2,1,0:T(8,128)}, u32[]{:S(2)}) copy-start(f32[36,36,512]{2,1,0:T(8,128)} %param.11) | copy-start | bytes 7962628
  88.3 6.0 %copy-start.5 = (f32[1,36,512]{2,1,0:T(8,128)S(1)}, f32[1,36,512]{2,1,0:T(8,128)}, u32[]{:S(2)}) copy-start(f32[1,36,512]{2,1,0:T(8,128)} %copy-done.4) | copy-start | bytes 221188
  88.3 6.0 %copy-start.7 = (f32[1,36,512]{2,1,0:T(8,128)S(1)}, f32[1,36,512]{2,1,0:T(8,128)}, u32[]{:S(2)}) copy-start(f32[1,36,512]{2,1,0:T(8,128)} %copy-done.6) | copy-start | bytes 221188
  90.4 4.5 %copy-start.3 = (bf16[20,2,40,512]{3,2,0,1:T(8,128)(2,1)}, bf16[20,2,40,512]{3,2,0,1:T(8,128)(2,1)S(1)}, u32[]{:S(2)}) copy-start(bf16[20,2,40,512]{3,2,0,1:T(8,128)(2,1)S(1)} %copy.40) | copy-start | bytes 4915204
  90.4 37.1 %collective-permute-start.4 = (bf16[2,800,512]{2,1,0:T(8,128)(2,1)S(1)}, bf16[2,800,512]{2,1,0:T(8,128)(2,1)S(1)}, u32[]{:S(2)}, u32[]{:S(2)}) collective-permute-start(bf16[2,800,512]{2,1,0:T(8,128)(2,1)S(1)} %bitcast.33), channel_id=1, source_target_pairs={{0,1},{1,0},{2,3},{3,2},{4,5},{5,4},{6,7},{7,6},{8,9},{9,8},{10,11... | collective-permute-start | bytes 4915208 | tf_op jit(solution)/shard_map/ppermute | solution.py:271
  127.5 1.1 copy-start.13
  189.5 34.9 %collective-permute-start.5 = (bf16[2,768,512]{2,1,0:T(8,128)(2,1)}, bf16[2,768,512]{2,1,0:T(8,128)(2,1)S(1)}, u32[]{:S(2)}, u32[]{:S(2)}) collective-permute-start(bf16[2,768,512]{2,1,0:T(8,128)(2,1)} %get-tuple-element.4.refs_0_), channel_id=1, source_target_pairs={{0,1},{1,0},{2,3},{3,2},{4,5},{5,4},{6,7},{7,6},{8,9},{9,8},{10,11... | collective-permute-start | bytes 4718600 | tf_op jit(solution)/shard_map/ppermute | solution.py:271
  224.4 1.1 copy-start.14

commit v2 on v0

v2 whole, which is shorter than its diff:
```python
import functools

import jax
import jax.numpy as jnp
from jax import lax
from jax.experimental import pallas as pl
from jax.experimental.pallas import tpu as pltpu
from jax.sharding import PartitionSpec as P

STEPS = 2
LANES = 128
GATES = 4 * LANES
F32 = jnp.float32
BF16 = jnp.bfloat16
VMEM = 60 * 2**20


def up_to(value, multiple):
    return -(-value // multiple) * multiple


def params():
    return pltpu.CompilerParams(vmem_limit_bytes=VMEM)


def input_weights_kernel(depth, blocks, w_ref, *refs):
    out_ref, wide_ref = refs[-2:]
    for j in range(blocks):
        lanes = slice(LANES * j, LANES * j + LANES)
        for b in range(3):
            wide_ref[b] = w_ref[0, b, :, :, lanes].astype(F32).reshape(depth * 4, LANES)
        for gate in range(4):
            out = slice(LANES * gate, LANES * gate + LANES)
            for b in range(3):
                rows = wide_ref[b, pl.ds(gate, depth, stride=4), :]
                out_ref[j, depth * b : depth * b + depth, out] = rows.astype(BF16)
        out_ref[j, 3 * depth :, :] = jnp.zeros((depth, GATES), BF16)


def input_weights(w_input, *after):
    _, depth, _, width = w_input.shape
    blocks = width // LANES
    return pl.pallas_call(
        functools.partial(input_weights_kernel, depth, blocks),
        grid=(3,),
        in_specs=[pl.BlockSpec((1, 3, depth, 4, width), lambda a: (a, 0, 0, 0, 0))]
        + [pl.BlockSpec(memory_space=pl.ANY)] * len(after),
        out_specs=pl.BlockSpec((blocks, 4 * depth, GATES), lambda a: (0, a, 0)),
        out_shape=jax.ShapeDtypeStruct((blocks, 12 * depth, GATES), BF16),
        scratch_shapes=[pltpu.VMEM((3, depth * 4, LANES), F32)],
        compiler_params=params(),
        cost_estimate=pl.CostEstimate(
            flops=0, bytes_accessed=48 * depth * 4 * width, transcendentals=0
        ),
        name="input_weights",
    )(w_input.reshape(3, 3, depth, 4, width), *after)


def sigmoid(x):
    return 0.5 * jnp.tanh(0.5 * x) + 0.5


def place(out_ref, origin, sizes, inner, rim_row, rim_col):
    rows, cols, stride = sizes
    for y in range(-origin, rows + origin):
        at = y + origin
        start = stride * (at // 2) + origin
        if y < 0:
            row = rim_row(0, y + 2)
        elif y >= rows:
            row = rim_row(1, y - rows)
        else:
            row = inner(y)
        out_ref[at % 2, start : start + cols, :] = row
    pairs = rows // 2 + origin
    for p in range(2):
        skip = (p + 2 - origin) // 2
        for k in range(origin):
            left = rim_col(0, 2 - origin + k, (p - origin) % 2)
            right = rim_col(1, k, (p - origin) % 2)
            out_ref[p, pl.ds(k, pairs, stride=stride), :] = left[skip : skip + pairs]
            at = origin + cols + k
            out_ref[p, pl.ds(at, pairs, stride=stride), :] = right[skip : skip + pairs]


def pass_kernel(dims, *refs):
    sizes, height, tiles, step, raw, first, final, into = dims
    rows, cols, stride = sizes
    fused = step == 0
    key_ref, refs = refs[0], list(refs[1:])
    take = lambda count: [refs.pop(0) for _ in range(count)]
    hidden_refs = take(3 if raw else 1)
    if first:
        frame_ref, frame_rows_ref, frame_cols_ref, w_ref, bias_ref = take(5)
    else:
        (before_ref,) = take(1)
    (u_ref,) = take(1)
    if fused:
        raw_ref = u_ref
        take(into)
    if final and step == 0:
        cell_in_ref, cell_rows_ref, cell_cols_ref, mask_ref = take(4)
    elif final:
        (cell_ref,) = take(1)
    if final:
        hidden_out, cell_out = take(2)
    else:
        (pre_ref,) = take(1)
    if fused:
        (u_ref,) = take(1)
    v_ref, wide_ref = take(2)
    if first:
        (x_ref,) = take(1)
    if final:
        (pre_ref,) = take(1)
    if final and step == 0:
        (cell_ref,) = take(1)
    if fused:
        (flat_ref,) = take(1)
    channels = v_ref.shape[2] // 3

    def build_x():
        inner = lambda y: frame_ref[y].astype(F32)
        rim_row = lambda side, k: frame_rows_ref[2 * side + k]
        rim_col = lambda side, k, p: frame_cols_ref[4 * side + 2 * k + p]
        place(wide_ref, 2 - step, sizes, inner, rim_row, rim_col)
        chunk = 48 if height % 48 == 0 else 16
        low = lax.broadcasted_iota(jnp.int32, (chunk, LANES), 1) < LANES // 2
        for q in range(2):
            for pair in range(2):
                for r in range(0, height, chunk):
                    start = stride * pair + r
                    at = [wide_ref[q, start + b : start + b + chunk, :] for b in range(3)]
                    turned = [pltpu.roll(value, LANES // 2, 1) for value in at]
                    if step == 0:
                        two, one = jnp.where(low, at[0], turned[1]), at[2]
                    else:
                        two, one = jnp.where(low, turned[0], at[1]), turned[2]
                    two, one = two.astype(BF16), one.astype(BF16)
                    rows = slice(r, r + chunk)
                    for p in range(2):
                        a = 2 * pair + q - p
                        if 0 <= a < 3:
                            x_ref[p, rows, 256 * a : 256 * a + LANES] = two
                            x_ref[p, rows, 256 * a + LANES : 256 * a + 256] = one

    def build_v(b, to):
        chunk = 48 if height % 48 == 0 else 16
        to = pl.ds(to, LANES)
        for r in range(0, height, chunk):
            near, far = slice(b + r, b + r + chunk), slice(stride + b + r, stride + b + r + chunk)
            d0, d1 = wide_ref[0, near, :], wide_ref[1, near, :]
            d2, d3 = wide_ref[0, far, :], wide_ref[1, far, :]
            rows = slice(r, r + chunk)
            v_ref[0, rows, to] = (d0 - d2).astype(BF16)
            v_ref[1, rows, to] = (d1 + d2).astype(BF16)
            v_ref[2, rows, to] = (d2 - d1).astype(BF16)
            v_ref[3, rows, to] = (d1 - d3).astype(BF16)

    def transform(b, c, chunk):
        rows = slice(c, c + chunk)
        for a in range(3):
            taken = raw_ref[a, b, rows, :, :].astype(F32)
            flat_ref[a, 4 * c : 4 * (c + chunk), :] = taken.reshape(4 * chunk, LANES)
        for gate in range(4):
            at = pl.ds(4 * c + gate, chunk, stride=4)
            g0, g1, g2 = [flat_ref[a, at, :] for a in range(3)]
            ends = g0 + g2
            out = slice(LANES * gate, LANES * gate + LANES)
            u_ref[0, 0, 0, b, rows, out] = (ends + g1).astype(BF16)
            u_ref[0, 0, 1, b, rows, out] = (ends - g1).astype(BF16)
            u_ref[0, 1, 0, b, rows, out] = g0.astype(BF16)
            u_ref[0, 1, 1, b, rows, out] = g2.astype(BF16)

    @pl.when(pl.program_id(0) == 0)
    def _():
        wide_ref[...] = jnp.zeros(wide_ref.shape, F32)
        if first:
            build_x()

        @pl.loop(0, channels // LANES)
        def _(j):
            lanes = pl.ds(pl.multiple_of(j * LANES, LANES), LANES)
            if raw:
                inner_ref, rows_ref, cols_ref = hidden_refs
                inner = lambda y: inner_ref[y, :, lanes].astype(F32)
                rim_row = lambda side, k: rows_ref[2 * side + k, :, lanes]
                rim_col = lambda side, k, p: cols_ref[4 * side + 2 * k + p, :, lanes]
                place(wide_ref, 2, sizes, inner, rim_row, rim_col)
            else:
                (hidden_ref,) = hidden_refs
                wide_ref[:, : hidden_ref.shape[1], :] = hidden_ref[:, :, lanes].astype(F32)
            for b in range(3):
                build_v(b, pl.multiple_of(b * channels + j * LANES, LANES))

    if final and step == 0:
        cell_ref[0] = jnp.zeros(cell_ref.shape[1:], F32)
        place(
            cell_ref.at[0],
            1,
            sizes,
            lambda y: cell_in_ref[y],
            lambda side, k: cell_rows_ref[2 * side] + cell_rows_ref[2 * side + 1],
            lambda side, k, p: cell_cols_ref[4 * side + p] + cell_cols_ref[4 * side + 2 + p],
        )

    def dot(a, b):
        return jnp.dot(a, b, preferred_element_type=F32)

    def gates(low, high, p, pre):
        m = slice(low, high)
        i, f, o, g = [pre[:, LANES * k : LANES * k + LANES] for k in range(4)]
        if step == 0:
            before = cell_ref[0, p, m, :]
        else:
            skip = 1 + stride * p
            before = cell_ref[0, 1 - p, low + skip : high + skip, :]
        cell = sigmoid(f) * before + sigmoid(i) * jnp.tanh(g)
        hidden = sigmoid(o) * jnp.tanh(cell)
        if step == 0:
            cell_out[0, p, m, :] = cell
            hidden_out[p, m, :] = jnp.where(mask_ref[p, m, :] > 0, hidden, 0).astype(BF16)
        else:
            for t in range(low // stride, high // stride):
                r = slice(t * stride - low, t * stride - low + cols)
                cell_out[2 * t + p] = cell[r]
                hidden_out[2 * t + p] = hidden[r].astype(BF16)

    chunk = 32
    groups = 3 if fused else 1
    depth = 3 * channels // groups
    if fused:
        for c in range(0, channels, chunk):
            transform(0, c, chunk)
    for group in range(groups):
        ready = group * depth
        waiting = []
        if fused and group < 2:
            waiting = [(group + 1, c, chunk) for c in range(0, channels, chunk)]
        share = -(-len(waiting) // (4 * len(tiles)))
        for low, high in tiles:
            m = slice(low, high)
            made = {}
            for k in (1, 2, 0, 3):
                place_of = {1: (0, 0), 2: (0, 1), 0: (1, 0), 3: (1, 1)}[k]
                if fused:
                    weights = u_ref[0, place_of[0], place_of[1], group]
                else:
                    weights = u_ref[0, place_of[0], place_of[1]].reshape(depth, GATES)
                made[k] = dot(v_ref[k, m, ready : ready + depth], weights)
                for _ in range(share):
                    if waiting:
                        transform(*waiting.pop(0))
            for p in range(2):
                if group > 0:
                    other = pre_ref[0, p, m, :]
                elif first:
                    bias = jnp.concatenate([bias_ref[k : k + 1, :] for k in range(4)], axis=1)
                    other = dot(x_ref[p, m, :], w_ref[0]) + bias
                else:
                    other = before_ref[0, p, m, :]
                both = made[1] - made[2] if p else made[1] + made[2]
                edge = -made[3] if p else made[0]
                pre = 0.5 * both + edge + other
                if final and group == groups - 1:
                    gates(low, high, p, pre)
                else:
                    pre_ref[0, p, m, :] = pre


def run_pass(step, sizes, half, hidden, u, frame=None, before=None, cell=None, mask=None, into=None):
    rows, cols, stride = sizes
    raw = isinstance(hidden, tuple)
    hiddens = hidden if raw else (hidden,)
    channels = hiddens[0].shape[2]
    first, final, fused = frame is not None, cell is not None, step == 0
    count = u.shape[4] // LANES if fused else u.shape[0]
    pairs = rows // 2 + (1 - step)
    height = up_to(pairs * stride, 16)
    middle = up_to(height // 2, 2 * stride if step else 16)
    tiles = ((0, middle), (middle, height))
    wide = up_to(max((rows // 2 + 2) * stride, height + stride + 2), 8)
    dims = (sizes, height, tiles, step, raw, first, final, int(into is not None))
    once = pl.Buffered(1)

    def whole(array):
        zeros = (0,) * array.ndim
        return pl.BlockSpec(array.shape, lambda n, k: zeros, pipeline_mode=once)

    def add(array, spec=None):
        args.append(array)
        in_specs.append(whole(array) if spec is None else spec)

    args, in_specs, aliases = [], [], {}
    for array in hiddens:
        add(array)
    if first:
        inner, rim_rows, rim_cols, w_in, biases = frame
        add(inner)
        add(rim_rows)
        add(rim_cols)
        add(w_in, pl.BlockSpec((1, w_in.shape[1], GATES), lambda n, k: (n, 0, 0)))
        add(biases, pl.BlockSpec((4, LANES), lambda n, k: (0, n)))
    else:
        add(before, pl.BlockSpec((1, 2, height, GATES), lambda n, k: (n, 0, 0, 0)))
    u_spec = pl.BlockSpec((1, 2, 2, 3, channels, GATES), lambda n, k: (n, 0, 0, 0, k[0], 0))
    if fused:
        add(u, pl.BlockSpec((3, 3, channels, 4, LANES), lambda n, k: (0, 0, k[0], 0, n)))
        if into is not None:
            aliases = {1 + len(args): 2 if final else 1}
            add(into, pl.BlockSpec(memory_space=pl.ANY))
    else:
        add(u, u_spec)
    if final and step == 0:
        for array in cell:
            add(array, pl.BlockSpec(array.shape[:2] + (LANES,), lambda n, k: (0, 0, n)))
        add(mask)
    elif final:
        add(cell, pl.BlockSpec((1,) + cell.shape[1:], lambda n, k: (n, 0, 0, 0)))
    scratch = [
        pltpu.VMEM((4, height, 3 * channels), BF16),
        pltpu.VMEM((2, wide, LANES), F32),
    ]
    if first:
        scratch.append(pltpu.VMEM((2, height, 6 * LANES), BF16))
    if final:
        scratch.append(pltpu.VMEM((1, 2, height, GATES), F32))
    if final and step == 0:
        scratch.append(pltpu.VMEM((1, 2, height, LANES), F32))
    if fused:
        scratch.append(pltpu.VMEM((3, 4 * channels, LANES), F32))
    if not final:
        out_specs = [pl.BlockSpec((1, 2, height, GATES), lambda n, k: (n, 0, 0, 0))]
        out_shape = [jax.ShapeDtypeStruct((count, 2, height, GATES), F32)]
    elif step == 0:
        out_specs = [
            pl.BlockSpec((2, height, LANES), lambda n, k: (0, 0, n)),
            pl.BlockSpec((1, 2, height, LANES), lambda n, k: (n, 0, 0, 0)),
        ]
        out_shape = [
            jax.ShapeDtypeStruct((2, height, count * LANES), BF16),
            jax.ShapeDtypeStruct((count, 2, height, LANES), F32),
        ]
    else:
        shape = (rows, cols, count * LANES)
        out_specs = [pl.BlockSpec((rows, cols, LANES), lambda n, k: (0, 0, n))] * 2
        out_shape = [jax.ShapeDtypeStruct(shape, BF16), jax.ShapeDtypeStruct(shape, F32)]
    if fused:
        out_specs.append(u_spec)
        out_shape.append(jax.ShapeDtypeStruct((count, 2, 2, 3, 2 * channels, GATES), BF16))
    return pl.pallas_call(
        functools.partial(pass_kernel, dims),
        grid_spec=pltpu.PrefetchScalarGridSpec(
            num_scalar_prefetch=1,
            grid=(count,),
            in_specs=in_specs,
            out_specs=out_specs,
            scratch_shapes=scratch,
        ),
        out_shape=out_shape,
        input_output_aliases=aliases,
        compiler_params=params(),
        cost_estimate=pl.CostEstimate(
            flops=2 * height * count * GATES * 12 * channels,
            bytes_accessed=24 * channels * count * GATES,
            transcendentals=height * count * LANES * 10,
        ),
        name="step%d" % step,
    )(half.reshape(1), *args)


def forward(x, axis):
    count = lax.axis_size(axis)
    return lax.ppermute(x, axis, [(i, i + 1) for i in range(count - 1)])


def backward(x, axis):
    count = lax.axis_size(axis)
    return lax.ppermute(x, axis, [(i + 1, i) for i in range(count - 1)])


def swapped(x):
    return lax.ppermute(x, "ch", [(0, 1), (1, 0)])


def split(x):
    high = lax.reduce_precision(x, 8, 7)
    return high.astype(BF16), (x - high).astype(BF16)


def row_pack(hidden, frames, cell, two, one):
    ends = jnp.stack(split(cell[one]))
    return jnp.concatenate([hidden[two : two + 2], frames[two : two + 2], ends], axis=2)


def col_pack(hidden, frames, cell, north, south, two, one):
    rows, _, width = hidden.shape
    main = width + frames.shape[2]
    ends = jnp.stack(split(cell[:, one]), axis=1)
    middle = jnp.concatenate([hidden[:, two : two + 2], frames[:, two : two + 2], ends], axis=2)
    none = jnp.zeros((1, 2, width), BF16)
    upper = jnp.concatenate([none, north[None, :, one, main:]], axis=0)
    lower = jnp.concatenate([south[None, :, one, main:], none], axis=0)
    upper = jnp.concatenate([north[:, two : two + 2, :main], upper], axis=2)
    lower = jnp.concatenate([south[:, two : two + 2, :main], lower], axis=2)
    strip = jnp.concatenate([upper, middle, lower], axis=0)
    strip = strip.reshape(rows // 2 + 2, 2, 2, -1).transpose(2, 1, 0, 3)
    return strip.reshape(4, rows // 2 + 2, -1)


def inside(rows, cols, stride, height):
    p = lax.broadcasted_iota(jnp.int32, (2, height, LANES), 0)
    flat = lax.broadcasted_iota(jnp.int32, (2, height, LANES), 1)
    y = 2 * (flat // stride) + p - 1 + lax.axis_index("sy") * rows
    x = flat % stride - 1
    wholly = (x <= cols) & (flat // stride <= rows // 2)
    x = x + lax.axis_index("sx") * cols
    ny, nx = rows * lax.axis_size("sy"), cols * lax.axis_size("sx")
    return ((y >= 0) & (y < ny) & (x >= 0) & (x < nx) & wholly).astype(F32)


def per_device(frames, w_input, w_hidden, biases, hidden_init, cell_init):
    rows, cols, width = hidden_init.shape
    main = width + frames.shape[2]
    stride = up_to(cols + 4, 8)
    sizes = (rows, cols, stride)
    count = lax.axis_size("ch")
    paired = count == 2
    gather = lambda x: lax.all_gather(x, "ch", axis=x.ndim - 1, tiled=True)
    other = swapped(hidden_init) if paired else gather(hidden_init)
    local = (hidden_init, frames, cell_init)
    to_south = row_pack(*local, rows - 2, rows - 1)
    to_north = row_pack(*local, 0, 0)
    north, south = forward(to_south, "sy"), backward(to_north, "sy")
    w_in = input_weights(w_input, to_south, to_north)
    to_east = col_pack(*local, north, south, cols - 2, cols - 1)
    to_west = col_pack(*local, north, south, 0, 0)
    west, east = forward(to_east, "sx"), backward(to_west, "sx")
    rim_rows, rim_cols = jnp.concatenate([north, south]), jnp.concatenate([west, east])
    length = rim_rows.shape[0] * rim_rows.shape[1]
    ring = jnp.concatenate(
        [rim_rows[:, :, :width].reshape(length, width), rim_cols[:, :, :width].reshape(-1, width)]
    )

    def unpacked(ring):
        ring = ring.astype(F32)
        return (
            ring[:length].reshape(rim_rows.shape[:2] + ring.shape[1:]),
            ring[length:].reshape(rim_cols.shape[:2] + ring.shape[1:]),
        )

    frame = (
        frames,
        rim_rows[:, :, width:main].astype(F32),
        rim_cols[:, :, width:main].astype(F32),
        w_in,
        biases,
    )
    cell = (cell_init, rim_rows[:, :, main:].astype(F32), rim_cols[:, :, main:].astype(F32))
    mask = inside(rows, cols, stride, up_to((rows // 2 + 1) * stride, 16))
    raw = (hidden_init,) + unpacked(ring)
    if paired:
        me = lax.axis_index("ch").astype(jnp.int32)
        halves = (me, 1 - me)
        hiddens = (raw, (other,) + unpacked(swapped(ring)))
    else:
        halves = (jnp.int32(0), jnp.int32(1))
        full = (other,) + unpacked(gather(ring))
        cut = other.shape[2] // 2
        hiddens = [tuple(x[:, :, k * cut : k * cut + cut] for x in full) for k in range(2)]
    w = w_hidden.reshape((3, 3) + w_hidden.shape[1:])
    before, u = run_pass(0, sizes, halves[0], hiddens[0], w, frame=frame)
    hidden, cell, u = run_pass(
        0, sizes, halves[1], hiddens[1], w, before=before, cell=cell, mask=mask, into=u
    )
    if paired:
        hiddens = (hidden, swapped(hidden))
    else:
        full = gather(hidden)
        hiddens = [full[:, :, k * cut : k * cut + cut] for k in range(2)]
    (before,) = run_pass(1, sizes, halves[0], hiddens[0], u, frame=frame)
    return tuple(run_pass(1, sizes, halves[1], hiddens[1], u, before=before, cell=cell))


def solution(mesh):
    in_specs = (
        P("sy", "sx", None),
        P(None, None, None, "ch"),
        P(None, None, None, "ch"),
        P(None, "ch"),
        P("sy", "sx", "ch"),
        P("sy", "sx", "ch"),
    )
    out_specs = (P("sy", "sx", "ch"), P("sy", "sx", "ch"))
    return jax.shard_map(
        per_device, mesh=mesh, in_specs=in_specs, out_specs=out_specs, check_vma=False
    )
```

time: 718 us -> 190 us (0.26); the launches traced: 709 us -> 189 us
  matrix products: 379 us -> 0 us
  local copies, waits for them, and re-layouts: 234 us -> 11.3 us
  Pallas kernels: 0 us -> 149 us
  other arithmetic: 37.1 us -> 6.21 us
  starting transfers between devices: 28.7 us -> 13.7 us
  between operations: 15.1 us -> 1.05 us
    dot_general x36 -> x0, matrix products: 379 us -> none  [taps_sum(): jnp.dot(window, kernels[tap], preferred_element_type=jnp.float32)]
    pallas_call x0 -> x5, Pallas kernels: none -> 149 us  [the longest x4 144 us: run_pass(): pl.pallas_call(functools.partial(pass_kernel, dims), grid_spec=pltpu.Pref...]
    reshape x38 -> x10, local copies, waits for them, and re-layouts: 112 us -> 3.36 us  [the longest x2 1.59 us: unpacked(): ring[length:].reshape(rim_cols.shape[:2] + ring.shape[1:])]
    slice x15 -> x13, local copies, waits for them, and re-layouts: 86.3 us -> 5.38 us  [the longest x1 1.38 us: col_pack(): ends = jnp.stack(split(cell[:, one]), axis=1)]
    unnamed x130 -> x17, local copies, waits for them, and re-layouts: 35 us -> 2.42 us
    concatenate x6 -> x8, other arithmetic: 28.2 us -> 0.23 us  [the longest x2 0.15 us: col_pack(): strip = jnp.concatenate([upper, middle, lower], axis=0)]
    ppermute x12 -> x7, starting transfers between devices: 28.6 us -> 13.7 us  [the longest x2 6.03 us: forward(): return lax.ppermute(x, axis, [(i, i + 1) for i in range(count - 1)])]
    all_gather x2 -> x0, waiting for transfers between devices: 13.9 us -> none  [per_device(): whole = lax.all_gather(hidden, 'ch', axis=2, tiled=True)]
  transfers between devices with their start and end apart: 14 -> 7, of which waited for: 1 -> 2; matrix products, arithmetic and copies ran while one was open for 37% -> 8% of each run, Pallas kernels for 0% -> 42%
where the time goes in v2:
time: 190 us; the launch traced here: 189 us
  Pallas kernels  149 us (78%)
  starting transfers between devices  13.7 us (7%)
  local copies, waits for them, and re-layouts  11.3 us (6%)
  waiting for transfers between devices  7.66 us (4%)
  other arithmetic  6.21 us (3%)
    pallas_call x4, Pallas kernels, run_pass(): pl.pallas_call(functools.partial(pass_kernel, dims), grid_spec=pltpu.Pref...  144 us
    ppermute x2, starting transfers between devices, forward(): return lax.ppermute(x, axis, [(i, i + 1) for i in range(count - 1)])  6.03 us
    ppermute x3, starting transfers between devices, swapped(): return lax.ppermute(x, 'ch', [(0, 1), (1, 0)])  5.06 us
    pallas_call x1, Pallas kernels, input_weights(): pl.pallas_call(functools.partial(input_weights_kernel, depth, blocks), gr...  4.55 us
    ppermute x3, waiting for transfers between devices, swapped(): return lax.ppermute(x, 'ch', [(0, 1), (1, 0)])  3.97 us
  transfers between devices with their start and end apart: 7, of which 2 were waited for; matrix products, arithmetic and copies ran while one was open for 8% of the time, Pallas kernels for 42%

profile of v2, /device:TPU:0, one launch (start us, length us, event | category | flops | bytes accessed | tf_op | source)
XLA Modules:
  0.0 188.7 jit_solution(17884180296334417193)
XLA Ops:
  0.6 3.0 %collective-permute-start = (bf16[36,36,512]{2,1,0:T(8,128)(2,1)}, bf16[36,36,512]{2,1,0:T(8,128)(2,1)S(1)}, u32[]{:S(2)}, u32[]{:S(2)}) collective-permute-start(bf16[36,36,512]{2,1,0:T(8,128)(2,1)} %refs_1_.1), channel_id=1, source_target_pairs={{0,1},{1,0},{2,3},{3,2},{4,5},{5,4},{6,7},{7,6},{8,9},{9,8},{10,11... | collective-permute-start | bytes 3981320 | tf_op jit(solution)/shard_map/ppermute | solution.py:383
  3.7 1.0 fusion.35
  4.6 0.8 fusion.37
  5.4 0.9 reduce-precision_convert_fusion.2
  6.4 0.0 copy-start.2
  6.4 1.5 collective-permute-start.1
  7.9 0.0 copy-start.1
  7.9 1.3 collective-permute-start.2
  9.2 1.0 fusion.36
  10.2 1.4 fusion.33
  11.6 1.2 fusion.34
  12.8 0.0 copy-done.2
  12.8 0.0 copy-done.1
  12.8 4.6 %input_weights.1.refs_7_.refs_5_ = bf16[4,768,512]{2,1,0:T(8,128)(2,1)} custom-call(bf16[3,3,64,4,512]{4,3,2,1,0:T(4,128)(2,1)} %bitcast.24, bf16[2,36,1152]{2,1,0:T(8,128)(2,1)} %copy-done.2, bf16[2,36,1152]{2,1,0:T(8,128)(2,1)} %copy-done.1), custom_call_target="tpu_custom_call" | custom-call | bytes 6291456 | tf_op jit(solution)/shard_map/input_weights/pallas_call | solution.py:43
  17.4 2.2 %fusion.13.refs_10_ = f32[2,768,128]{2,1,0:T(8,128)} fusion(s32[]{:T(128)S(6)} %mul.15, s32[768]{0:T(1024)S(1)} %get-tuple-element.49, s32[768]{0:T(1024)S(1)} %get-tuple-element.50, s32[]{:T(128)S(6)} %mul.14, s32[768]{0:T(1024)S(1)} %get-tuple-element.48, s32[768]{0:T(1024)S(1)} %get-tuple-element.51, pred[768]{0:T(1024)(128)(4,1)S(1)} %get-tuple-element.52, ...), kind=kLoop, calls=%fused_computation.16 | loop fusion | flops 3932160 | bytes 800264 | tf_op jit(solution)/shard_map/convert_element_type | solution.py:419
  19.6 0.0 collective-permute-done.1
  19.7 0.0 collective-permute-done.2
  19.8 0.1 pad_maximum_fusion.1
  19.9 0.1 reshape.52
  20.0 0.1 pad_maximum_fusion
  20.1 0.1 reshape.50
  20.3 0.8 slice_convert_fusion.1
  21.1 1.3 collective-permute-start.4
  22.4 4.6 %collective-permute-start.3 = (bf16[4,20,1152]{2,1,0:T(8,128)(2,1)S(1)}, bf16[4,20,1152]{2,1,0:T(8,128)(2,1)S(1)}, u32[]{:S(2)}, u32[]{:S(2)}) collective-permute-start(bf16[4,20,1152]{2,1,0:T(8,128)(2,1)S(1)} %bitcast.26), channel_id=1, source_target_pairs={{0,2},{2,4},{4,6},{1,3},{3,5},{5,7},{8,10},{10,12},{12,14},{9,11},... | collective-permute-start | bytes 552968 | tf_op jit(solution)/shard_map/ppermute | solution.py:374
  27.0 0.6 slice_convert_fusion.3.refs_5_.refs_3_
  27.6 3.7 %collective-permute-done.3 = bf16[4,20,1152]{2,1,0:T(8,128)(2,1)S(1)} collective-permute-done((bf16[4,20,1152]{2,1,0:T(8,128)(2,1)S(1)}, bf16[4,20,1152]{2,1,0:T(8,128)(2,1)S(1)}, u32[]{:S(2)}, u32[]{:S(2)}) %collective-permute-start.3) | collective-permute-done | bytes 184352 | tf_op jit(solution)/shard_map/ppermute | solution.py:374
  31.3 0.0 collective-permute-done.4
  31.3 0.6 slice_convert_fusion.2.refs_6_.refs_4_
  32.0 0.8 slice_convert_fusion
  32.9 0.1 collective-permute-start.5
  33.0 0.8 reshape.58.refs_2_
  33.8 0.8 reshape.59.refs_3_
  34.6 43.8 %step0.2 = (f32[4,2,768,512]{3,2,1,0:T(8,128)}, bf16[4,2,2,3,1024,512]{5,4,3,2,1,0:T(8,128)(2,1)}) custom-call(s32[1]{0:T(128)} %bitcast.5.refs_0_, bf16[36,36,512]{2,1,0:T(8,128)(2,1)} %refs_1_.1, f32[4,36,512]{2,1,0:T(8,128)} %reshape.58.refs_2_, f32[8,20,512]{2,1,0:T(8,128)} %reshape.59.refs_3_, bf16[36,36,128]{2,1,0:T(8,128)(2,1)} %refs_2_.1, ...), custom_call_target="tpu_custom_call" | custom-call | flops 19327352832 | bytes 25165824 | tf_op jit(solution)/shard_map/step0/pallas_call | solution.py:351
  78.4 0.0 collective-permute-done.5
  78.4 0.8 reshape.55.refs_2_
  79.2 0.8 reshape.56.refs_3_
  80.0 0.0 collective-permute-done.refs_1_
  80.0 0.0 copy-start
  80.0 1.1 copy-done
  81.1 42.1 %step0.3 = (bf16[2,768,512]{2,1,0:T(8,128)(2,1)}, f32[4,2,768,128]{3,2,1,0:T(8,128)}, bf16[4,2,2,3,1024,512]{5,4,3,2,1,0:T(8,128)(2,1)}) custom-call(s32[1]{0:T(128)} %bitcast.refs_0_, bf16[36,36,512]{2,1,0:T(8,128)(2,1)} %copy-done, f32[4,36,512]{2,1,0:T(8,128)} %reshape.55.refs_2_, ...), custom_call_target="tpu_custom_call", output_to_operand_aliasing={{2}: (6, {})} | custom-call | flops 19327352832 | bytes 25165824 | tf_op jit(solution)/shard_map/step0/pallas_call | solution.py:351
  123.3 1.9 %collective-permute-start.6 = (bf16[2,768,512]{2,1,0:T(8,128)(2,1)}, bf16[2,768,512]{2,1,0:T(8,128)(2,1)S(1)}, u32[]{:S(2)}, u32[]{:S(2)}) collective-permute-start(bf16[2,768,512]{2,1,0:T(8,128)(2,1)} %get-tuple-element.9.refs_1_), channel_id=1, source_target_pairs={{0,1},{1,0},{2,3},{3,2},{4,5},{5,4},{6,7},{7,6},{8,9},{9,8},{10,11... | collective-permute-start | bytes 4718600 | tf_op jit(solution)/shard_map/ppermute | solution.py:383
  125.2 31.1 %step1.2.refs_2_ = f32[4,2,720,512]{3,2,1,0:T(8,128)} custom-call(s32[1]{0:T(128)} %bitcast.5.refs_0_, bf16[2,768,512]{2,1,0:T(8,128)(2,1)} %get-tuple-element.9.refs_1_, bf16[36,36,128]{2,1,0:T(8,128)(2,1)} %refs_2_.1, f32[4,36,128]{2,1,0:T(8,128)} %slice_convert_fusion.3.refs_5_.refs_3_, f32[8,20,128]{2,1,0:T(8,128)} %slice_convert_fusion.2.refs_6_.refs_4_, ...), custom_call_target="tpu_custom_call" | custom-call | flops 18119393280 | bytes 25165824 | tf_op jit(solution)/shard_map/step1/pallas_call | solution.py:351
  156.2 4.0 %collective-permute-done.6.refs_1_ = bf16[2,768,512]{2,1,0:T(8,128)(2,1)S(1)} collective-permute-done((bf16[2,768,512]{2,1,0:T(8,128)(2,1)}, bf16[2,768,512]{2,1,0:T(8,128)(2,1)S(1)}, u32[]{:S(2)}, u32[]{:S(2)}) %collective-permute-start.6) | collective-permute-done | bytes 1572896 | tf_op jit(solution)/shard_map/ppermute | solution.py:383
  160.2 0.0 copy-start.3
  160.2 1.2 copy-done.3
  161.4 27.2 %step1.3 = (bf16[36,36,512]{2,1,0:T(8,128)(2,1)}, f32[36,36,512]{2,1,0:T(8,128)}) custom-call(s32[1]{0:T(128)} %bitcast.refs_0_, bf16[2,768,512]{2,1,0:T(8,128)(2,1)} %copy-done.3, f32[4,2,720,512]{3,2,1,0:T(8,128)} %step1.2.refs_2_, bf16[4,2,2,3,1024,512]{5,4,3,2,1,0:T(8,128)(2,1)} %get-tuple-element.10.refs_7_.refs_3_, ...), custom_call_target="tpu_custom_call" | custom-call | flops 18119393280 | bytes 25165824 | tf_op jit(solution)/shard_map/step1/pallas_call | solution.py:351
  (38 shorter events, 0.6 us)
Async XLA Ops:
  0.6 79.4 %collective-permute-start = (bf16[36,36,512]{2,1,0:T(8,128)(2,1)}, bf16[36,36,512]{2,1,0:T(8,128)(2,1)S(1)}, u32[]{:S(2)}, u32[]{:S(2)}) collective-permute-start(bf16[36,36,512]{2,1,0:T(8,128)(2,1)} %refs_1_.1), channel_id=1, source_target_pairs={{0,1},{1,0},{2,3},{3,2},{4,5},{5,4},{6,7},{7,6},{8,9},{9,8},{10,11... | collective-permute-start | bytes 3981320 | tf_op jit(solution)/shard_map/ppermute | solution.py:383
  6.4 6.5 %copy-start.2 = (bf16[2,36,1152]{2,1,0:T(8,128)(2,1)}, bf16[2,36,1152]{2,1,0:T(8,128)(2,1)S(1)}, u32[]{:S(2)}) copy-start(bf16[2,36,1152]{2,1,0:T(8,128)(2,1)S(1)} %maximum_maximum_fusion.refs_0_) | copy-start | bytes 497668
  6.4 13.2 %collective-permute-start.1 = (bf16[2,36,1152]{2,1,0:T(8,128)(2,1)S(1)}, bf16[2,36,1152]{2,1,0:T(8,128)(2,1)S(1)}, u32[]{:S(2)}, u32[]{:S(2)}) collective-permute-start(bf16[2,36,1152]{2,1,0:T(8,128)(2,1)S(1)} %maximum_maximum_fusion.refs_0_), channel_id=1, source_target_pairs={{0,8},{8,16},{16,24},{1,9},{9,17},{17,25},{2,10},{10,18},{18,26},{... | collective-permute-start | bytes 497672 | tf_op jit(solution)/shard_map/ppermute | solution.py:374
  7.9 5.0 %copy-start.1 = (bf16[2,36,1152]{2,1,0:T(8,128)(2,1)}, bf16[2,36,1152]{2,1,0:T(8,128)(2,1)S(1)}, u32[]{:S(2)}) copy-start(bf16[2,36,1152]{2,1,0:T(8,128)(2,1)S(1)} %maximum_maximum_fusion.1.refs_1_) | copy-start | bytes 497668
  7.9 11.8 %collective-permute-start.2 = (bf16[2,36,1152]{2,1,0:T(8,128)(2,1)S(1)}, bf16[2,36,1152]{2,1,0:T(8,128)(2,1)S(1)}, u32[]{:S(2)}, u32[]{:S(2)}) collective-permute-start(bf16[2,36,1152]{2,1,0:T(8,128)(2,1)S(1)} %maximum_maximum_fusion.1.refs_1_), channel_id=1, source_target_pairs={{8,0},{16,8},{24,16},{9,1},{17,9},{25,17},{10,2},{18,10},{26,18},{... | collective-permute-start | bytes 497672 | tf_op jit(solution)/shard_map/ppermute | solution.py:379
  21.1 10.2 %collective-permute-start.4 = (bf16[4,20,1152]{2,1,0:T(8,128)(2,1)S(1)}, bf16[4,20,1152]{2,1,0:T(8,128)(2,1)S(1)}, u32[]{:S(2)}, u32[]{:S(2)}) collective-permute-start(bf16[4,20,1152]{2,1,0:T(8,128)(2,1)S(1)} %bitcast.25), channel_id=1, source_target_pairs={{2,0},{4,2},{6,4},{3,1},{5,3},{7,5},{10,8},{12,10},{14,12},{11,9},... | collective-permute-start | bytes 552968 | tf_op jit(solution)/shard_map/ppermute | solution.py:379
  22.4 8.9 %collective-permute-start.3 = (bf16[4,20,1152]{2,1,0:T(8,128)(2,1)S(1)}, bf16[4,20,1152]{2,1,0:T(8,128)(2,1)S(1)}, u32[]{:S(2)}, u32[]{:S(2)}) collective-permute-start(bf16[4,20,1152]{2,1,0:T(8,128)(2,1)S(1)} %bitcast.26), channel_id=1, source_target_pairs={{0,2},{2,4},{4,6},{1,3},{3,5},{5,7},{8,10},{10,12},{12,14},{9,11},... | collective-permute-start | bytes 552968 | tf_op jit(solution)/shard_map/ppermute | solution.py:374
  32.9 45.5 %collective-permute-start.5 = (bf16[304,512]{1,0:T(8,128)(2,1)S(1)}, bf16[304,512]{1,0:T(8,128)(2,1)S(1)}, u32[]{:S(2)}, u32[]{:S(2)}) collective-permute-start(bf16[304,512]{1,0:T(8,128)(2,1)S(1)} %constant_dynamic-update-slice_fusion.4), channel_id=1, source_target_pairs={{0,1},{1,0},{2,3},{3,2},{4,5},{5,4},{6,7},{7,6},{8,9},{9,8},{10,11... | collective-permute-start | bytes 933896 | tf_op jit(solution)/shard_map/ppermute | solution.py:383
  80.0 1.1 copy-start
  123.3 37.0 %collective-permute-start.6 = (bf16[2,768,512]{2,1,0:T(8,128)(2,1)}, bf16[2,768,512]{2,1,0:T(8,128)(2,1)S(1)}, u32[]{:S(2)}, u32[]{:S(2)}) collective-permute-start(bf16[2,768,512]{2,1,0:T(8,128)(2,1)} %get-tuple-element.9.refs_1_), channel_id=1, source_target_pairs={{0,1},{1,0},{2,3},{3,2},{4,5},{5,4},{6,7},{7,6},{8,9},{9,8},{10,11... | collective-permute-start | bytes 4718600 | tf_op jit(solution)/shard_map/ppermute | solution.py:383
  160.2 1.2 copy-start.3

commit v3 on v2

--- a/solution.py
+++ b/solution.py
@@ -89,9 +89,10 @@
     fused = step == 0
     key_ref, refs = refs[0], list(refs[1:])
     take = lambda count: [refs.pop(0) for _ in range(count)]
-    hidden_refs = take(3 if raw else 1)
+    hidden_refs = take(5 if raw else 1)
     if first:
-        frame_ref, frame_rows_ref, frame_cols_ref, w_ref, bias_ref = take(5)
+        frame_refs = take(5)
+        w_ref, bias_ref = take(2)
     else:
         (before_ref,) = take(1)
     (u_ref,) = take(1)
@@ -99,7 +100,7 @@
         raw_ref = u_ref
         take(into)
     if final and step == 0:
-        cell_in_ref, cell_rows_ref, cell_cols_ref, mask_ref = take(4)
+        cell_refs = take(5)
     elif final:
         (cell_ref,) = take(1)
     if final:
@@ -114,16 +115,21 @@
     if final:
         (pre_ref,) = take(1)
     if final and step == 0:
-        (cell_ref,) = take(1)
+        cell_ref, mask_ref = take(2)
     if fused:
         (flat_ref,) = take(1)
     channels = v_ref.shape[2] // 3
 
+    def surrounded(tile_refs, lanes):
+        inner_ref, rows_refs, cols_refs = tile_refs[0], tile_refs[1:3], tile_refs[3:5]
+        return (
+            lambda y: inner_ref[y, :, lanes].astype(F32),
+            lambda side, k: rows_refs[side][k, :, lanes].astype(F32),
+            lambda side, k, p: cols_refs[side][2 * k + p, :, lanes].astype(F32),
+        )
+
     def build_x():
-        inner = lambda y: frame_ref[y].astype(F32)
-        rim_row = lambda side, k: frame_rows_ref[2 * side + k]
-        rim_col = lambda side, k, p: frame_cols_ref[4 * side + 2 * k + p]
-        place(wide_ref, 2 - step, sizes, inner, rim_row, rim_col)
+        place(wide_ref, 2 - step, sizes, *surrounded(frame_refs, slice(None)))
         chunk = 48 if height % 48 == 0 else 16
         low = lax.broadcasted_iota(jnp.int32, (chunk, LANES), 1) < LANES // 2
         for q in range(2):
@@ -182,26 +188,38 @@
         def _(j):
             lanes = pl.ds(pl.multiple_of(j * LANES, LANES), LANES)
             if raw:
-                inner_ref, rows_ref, cols_ref = hidden_refs
-                inner = lambda y: inner_ref[y, :, lanes].astype(F32)
-                rim_row = lambda side, k: rows_ref[2 * side + k, :, lanes]
-                rim_col = lambda side, k, p: cols_ref[4 * side + 2 * k + p, :, lanes]
-                place(wide_ref, 2, sizes, inner, rim_row, rim_col)
+                place(wide_ref, 2, sizes, *surrounded(hidden_refs, lanes))
             else:
                 (hidden_ref,) = hidden_refs
                 wide_ref[:, : hidden_ref.shape[1], :] = hidden_ref[:, :, lanes].astype(F32)
             for b in range(3):
                 build_v(b, pl.multiple_of(b * channels + j * LANES, LANES))
 
+        if final and step == 0:
+            mask_ref[...] = jnp.zeros(mask_ref.shape, F32)
+            edge = lambda k, length: jnp.where(key_ref[2 + k] > 0, jnp.ones((length, LANES), F32), 0)
+            place(
+                mask_ref,
+                1,
+                sizes,
+                lambda y: jnp.ones((cols, LANES), F32),
+                lambda side, k: edge(side, cols),
+                lambda side, k, p: edge(2 + side, rows // 2 + 2),
+            )
+            low, high = slice(0, stride), slice(rows // 2 * stride, rows // 2 * stride + stride)
+            mask_ref[0, low, :] = jnp.where(key_ref[2] > 0, mask_ref[0, low, :], 0)
+            mask_ref[1, high, :] = jnp.where(key_ref[3] > 0, mask_ref[1, high, :], 0)
+
     if final and step == 0:
         cell_ref[0] = jnp.zeros(cell_ref.shape[1:], F32)
+        inner, rim_row, rim_col = surrounded(cell_refs, slice(None))
         place(
             cell_ref.at[0],
             1,
             sizes,
-            lambda y: cell_in_ref[y],
-            lambda side, k: cell_rows_ref[2 * side] + cell_rows_ref[2 * side + 1],
-            lambda side, k, p: cell_cols_ref[4 * side + p] + cell_cols_ref[4 * side + 2 + p],
+            inner,
+            lambda side, k: rim_row(side, 0) + rim_row(side, 1),
+            lambda side, k, p: rim_col(side, 0, p) + rim_col(side, 1, p),
         )
 
     def dot(a, b):
@@ -268,7 +286,7 @@
                     pre_ref[0, p, m, :] = pre
 
 
-def run_pass(step, sizes, half, hidden, u, frame=None, before=None, cell=None, mask=None, into=None):
+def run_pass(step, sizes, key, which, hidden, u, frame=None, before=None, cell=None, into=None):
     rows, cols, stride = sizes
     raw = isinstance(hidden, tuple)
     hiddens = hidden if raw else (hidden,)
@@ -293,28 +311,30 @@
 
     args, in_specs, aliases = [], [], {}
     for array in hiddens:
-        add(array)
+        block = array.shape[:2] + (channels,)
+        add(array, pl.BlockSpec(block, lambda n, k: (0, 0, 0), pipeline_mode=once))
     if first:
-        inner, rim_rows, rim_cols, w_in, biases = frame
+        inner, *rims, w_in, biases = frame
         add(inner)
-        add(rim_rows)
-        add(rim_cols)
+        for array in rims:
+            block = array.shape[:2] + (LANES,)
+            add(array, pl.BlockSpec(block, lambda n, k: (0, 0, count), pipeline_mode=once))
         add(w_in, pl.BlockSpec((1, w_in.shape[1], GATES), lambda n, k: (n, 0, 0)))
         add(biases, pl.BlockSpec((4, LANES), lambda n, k: (0, n)))
     else:
         add(before, pl.BlockSpec((1, 2, height, GATES), lambda n, k: (n, 0, 0, 0)))
-    u_spec = pl.BlockSpec((1, 2, 2, 3, channels, GATES), lambda n, k: (n, 0, 0, 0, k[0], 0))
-    if fused:
-        add(u, pl.BlockSpec((3, 3, channels, 4, LANES), lambda n, k: (0, 0, k[0], 0, n)))
+    u_spec = pl.BlockSpec((1, 2, 2, 3, channels, GATES), lambda n, k: (n, 0, 0, 0, k[which], 0))
+    if fused:
+        add(u, pl.BlockSpec((3, 3, channels, 4, LANES), lambda n, k: (0, 0, k[which], 0, n)))
         if into is not None:
             aliases = {1 + len(args): 2 if final else 1}
             add(into, pl.BlockSpec(memory_space=pl.ANY))
     else:
         add(u, u_spec)
     if final and step == 0:
-        for array in cell:
-            add(array, pl.BlockSpec(array.shape[:2] + (LANES,), lambda n, k: (0, 0, n)))
-        add(mask)
+        for array, base in zip(cell, (0,) + (count + 1,) * 4):
+            block = array.shape[:2] + (LANES,)
+            add(array, pl.BlockSpec(block, lambda n, k, base=base: (0, 0, base + n)))
     elif final:
         add(cell, pl.BlockSpec((1,) + cell.shape[1:], lambda n, k: (n, 0, 0, 0)))
     scratch = [
@@ -327,6 +347,7 @@
         scratch.append(pltpu.VMEM((1, 2, height, GATES), F32))
     if final and step == 0:
         scratch.append(pltpu.VMEM((1, 2, height, LANES), F32))
+        scratch.append(pltpu.VMEM((2, height, LANES), F32))
     if fused:
         scratch.append(pltpu.VMEM((3, 4 * channels, LANES), F32))
     if not final:
@@ -366,7 +387,7 @@
             transcendentals=height * count * LANES * 10,
         ),
         name="step%d" % step,
-    )(half.reshape(1), *args)
+    )(key, *args)
 
 
 def forward(x, axis):
@@ -408,20 +429,8 @@
     return strip.reshape(4, rows // 2 + 2, -1)
 
 
-def inside(rows, cols, stride, height):
-    p = lax.broadcasted_iota(jnp.int32, (2, height, LANES), 0)
-    flat = lax.broadcasted_iota(jnp.int32, (2, height, LANES), 1)
-    y = 2 * (flat // stride) + p - 1 + lax.axis_index("sy") * rows
-    x = flat % stride - 1
-    wholly = (x <= cols) & (flat // stride <= rows // 2)
-    x = x + lax.axis_index("sx") * cols
-    ny, nx = rows * lax.axis_size("sy"), cols * lax.axis_size("sx")
-    return ((y >= 0) & (y < ny) & (x >= 0) & (x < nx) & wholly).astype(F32)
-
-
 def per_device(frames, w_input, w_hidden, biases, hidden_init, cell_init):
     rows, cols, width = hidden_init.shape
-    main = width + frames.shape[2]
     stride = up_to(cols + 4, 8)
     sizes = (rows, cols, stride)
     count = lax.axis_size("ch")
@@ -432,54 +441,37 @@
     to_south = row_pack(*local, rows - 2, rows - 1)
     to_north = row_pack(*local, 0, 0)
     north, south = forward(to_south, "sy"), backward(to_north, "sy")
-    w_in = input_weights(w_input, to_south, to_north)
     to_east = col_pack(*local, north, south, cols - 2, cols - 1)
     to_west = col_pack(*local, north, south, 0, 0)
     west, east = forward(to_east, "sx"), backward(to_west, "sx")
-    rim_rows, rim_cols = jnp.concatenate([north, south]), jnp.concatenate([west, east])
-    length = rim_rows.shape[0] * rim_rows.shape[1]
-    ring = jnp.concatenate(
-        [rim_rows[:, :, :width].reshape(length, width), rim_cols[:, :, :width].reshape(-1, width)]
-    )
-
-    def unpacked(ring):
-        ring = ring.astype(F32)
-        return (
-            ring[:length].reshape(rim_rows.shape[:2] + ring.shape[1:]),
-            ring[length:].reshape(rim_cols.shape[:2] + ring.shape[1:]),
-        )
-
-    frame = (
-        frames,
-        rim_rows[:, :, width:main].astype(F32),
-        rim_cols[:, :, width:main].astype(F32),
-        w_in,
-        biases,
-    )
-    cell = (cell_init, rim_rows[:, :, main:].astype(F32), rim_cols[:, :, main:].astype(F32))
-    mask = inside(rows, cols, stride, up_to((rows // 2 + 1) * stride, 16))
-    raw = (hidden_init,) + unpacked(ring)
+    w_in = input_weights(w_input, to_east, to_west)
+    rims = (north, south, west, east)
+    frame = (frames, *rims, w_in, biases)
+    cell = (cell_init, *rims)
     if paired:
         me = lax.axis_index("ch").astype(jnp.int32)
         halves = (me, 1 - me)
-        hiddens = (raw, (other,) + unpacked(swapped(ring)))
+        hiddens = ((hidden_init, *rims), (other, *[swapped(rim) for rim in rims]))
     else:
         halves = (jnp.int32(0), jnp.int32(1))
-        full = (other,) + unpacked(gather(ring))
+        full = [other] + [gather(rim[:, :, :width]) for rim in rims]
         cut = other.shape[2] // 2
         hiddens = [tuple(x[:, :, k * cut : k * cut + cut] for x in full) for k in range(2)]
+    y, x = lax.axis_index("sy"), lax.axis_index("sx")
+    beside = [y > 0, y < lax.axis_size("sy") - 1, x > 0, x < lax.axis_size("sx") - 1]
+    key = jnp.stack(list(halves) + [b.astype(jnp.int32) for b in beside])
     w = w_hidden.reshape((3, 3) + w_hidden.shape[1:])
-    before, u = run_pass(0, sizes, halves[0], hiddens[0], w, frame=frame)
+    before, u = run_pass(0, sizes, key, 0, hiddens[0], w, frame=frame)
     hidden, cell, u = run_pass(
-        0, sizes, halves[1], hiddens[1], w, before=before, cell=cell, mask=mask, into=u
+        0, sizes, key, 1, hiddens[1], w, before=before, cell=cell, into=u
     )
     if paired:
         hiddens = (hidden, swapped(hidden))
     else:
         full = gather(hidden)
         hiddens = [full[:, :, k * cut : k * cut + cut] for k in range(2)]
-    (before,) = run_pass(1, sizes, halves[0], hiddens[0], u, frame=frame)
-    return tuple(run_pass(1, sizes, halves[1], hiddens[1], u, before=before, cell=cell))
+    (before,) = run_pass(1, sizes, key, 0, hiddens[0], u, frame=frame)
+    return tuple(run_pass(1, sizes, key, 1, hiddens[1], u, before=before, cell=cell))
 
 
 def solution(mesh):

time: 190 us -> 184 us (0.968)
  other arithmetic: 6.21 us -> 1.21 us
  Pallas kernels: 149 us -> 152 us
  waiting for transfers between devices: 7.66 us -> 4.77 us
  local copies, waits for them, and re-layouts: 11.3 us -> 8.59 us
  starting transfers between devices: 13.7 us -> 16.2 us
    convert_element_type x5 -> x0, other arithmetic: 4.98 us -> none  [the longest x1 2.16 us: inside(): return ((y >= 0) & (y < ny) & (x >= 0) & (x < nx) & wholly).astype(F32)]
    ppermute x2, waiting for transfers between devices: 3.68 us -> 0.01 us  [forward(): return lax.ppermute(x, axis, [(i, i + 1) for i in range(count - 1)])]
    pallas_call x4, Pallas kernels: 144 us -> 147 us  [run_pass(): pl.pallas_call(functools.partial(pass_kernel, dims), grid_spec=pltpu.Pref...]
    reshape x6 -> x0, local copies, waits for them, and re-layouts: 3.17 us -> none  [the longest x2 1.59 us: unpacked(): ring[length:].reshape(rim_cols.shape[:2] + ring.shape[1:])]
    ppermute x3 -> x6, starting transfers between devices: 5.06 us -> 6.64 us  [swapped(): return lax.ppermute(x, 'ch', [(0, 1), (1, 0)])]
    ppermute x3 -> x6, waiting for transfers between devices: 3.97 us -> 4.41 us  [swapped(): return lax.ppermute(x, 'ch', [(0, 1), (1, 0)])]
  transfers between devices with their start and end apart: 7 -> 10, of which waited for: 2 -> 2; matrix products, arithmetic and copies ran while one was open for 8% -> 2% of each run, Pallas kernels for 42% -> 44%
where the time goes in v3:
time: 184 us
  Pallas kernels  152 us (83%)
  starting transfers between devices  16.2 us (9%)
  local copies, waits for them, and re-layouts  8.59 us (5%)
  waiting for transfers between devices  4.77 us (3%)
    pallas_call x4, Pallas kernels, run_pass(): pl.pallas_call(functools.partial(pass_kernel, dims), grid_spec=pltpu.Pref...  147 us
    ppermute x2, starting transfers between devices, forward(): return lax.ppermute(x, axis, [(i, i + 1) for i in range(count - 1)])  6.99 us
    ppermute x6, starting transfers between devices, swapped(): return lax.ppermute(x, 'ch', [(0, 1), (1, 0)])  6.64 us
    pallas_call x1, Pallas kernels, input_weights(): pl.pallas_call(functools.partial(input_weights_kernel, depth, blocks), gr...  4.53 us
    ppermute x6, waiting for transfers between devices, swapped(): return lax.ppermute(x, 'ch', [(0, 1), (1, 0)])  4.41 us
  transfers between devices with their start and end apart: 10, of which 2 were waited for; matrix products, arithmetic and copies ran while one was open for 2% of the time, Pallas kernels for 44%

profile of v3, /device:TPU:0, one launch (start us, length us, event | category | flops | bytes accessed | tf_op | source)
XLA Modules:
  0.0 183.8 jit_solution(6168587360857486068)
XLA Ops:
  0.6 0.8 fusion.16
  1.4 0.9 reduce-precision_convert_fusion.2
  2.3 0.9 fusion.14
  3.3 2.4 %collective-permute-start.1 = (bf16[2,36,1152]{2,1,0:T(8,128)(2,1)S(1)}, bf16[2,36,1152]{2,1,0:T(8,128)(2,1)S(1)}, u32[]{:S(2)}, u32[]{:S(2)}) collective-permute-start(bf16[2,36,1152]{2,1,0:T(8,128)(2,1)S(1)} %maximum_maximum_fusion), channel_id=1, source_target_pairs={{0,8},{8,16},{16,24},{1,9},{9,17},{17,25},{2,10},{10,18},{18,26},{... | collective-permute-start | bytes 497672 | tf_op jit(solution)/shard_map/ppermute | solution.py:395
  5.7 1.3 collective-permute-start.3
  7.0 1.0 fusion.15
  8.0 1.4 fusion.12
  9.3 1.2 fusion.13
  10.6 0.0 collective-permute-done.1.refs_2_.refs_7_.refs_10_.refs_3_
  10.6 0.0 copy-start.5
  10.8 0.4 collective-permute-done.3.refs_3_.refs_8_.refs_11_.refs_4_
  11.1 0.0 copy-start.6
  11.2 0.1 pad_maximum_fusion.1
  11.3 0.1 reshape.24
  11.4 0.1 pad_maximum_fusion
  11.5 0.1 reshape.22
  11.6 0.0 copy-start.3
  11.6 0.0 copy-start.4
  11.7 1.3 collective-permute-start.7
  13.0 4.6 %collective-permute-start.5 = (bf16[4,20,1152]{2,1,0:T(8,128)(2,1)S(1)}, bf16[4,20,1152]{2,1,0:T(8,128)(2,1)S(1)}, u32[]{:S(2)}, u32[]{:S(2)}) collective-permute-start(bf16[4,20,1152]{2,1,0:T(8,128)(2,1)S(1)} %bitcast.29), channel_id=1, source_target_pairs={{0,2},{2,4},{4,6},{1,3},{3,5},{5,7},{8,10},{10,12},{12,14},{9,11},... | collective-permute-start | bytes 552968 | tf_op jit(solution)/shard_map/ppermute | solution.py:395
  17.6 2.0 %collective-permute-start = (bf16[36,36,512]{2,1,0:T(8,128)(2,1)}, bf16[36,36,512]{2,1,0:T(8,128)(2,1)S(1)}, u32[]{:S(2)}, u32[]{:S(2)}) collective-permute-start(bf16[36,36,512]{2,1,0:T(8,128)(2,1)} %refs_1_.1), channel_id=1, source_target_pairs={{0,1},{1,0},{2,3},{3,2},{4,5},{5,4},{6,7},{7,6},{8,9},{9,8},{10,11... | collective-permute-start | bytes 3981320 | tf_op jit(solution)/shard_map/ppermute | solution.py:404
  19.6 0.6 stack.63.refs_0_
  20.2 0.0 copy-done.3
  20.2 0.0 copy-done.4
  20.2 4.5 %input_weights.1.refs_11_.refs_7_ = bf16[4,768,512]{2,1,0:T(8,128)(2,1)} custom-call(bf16[3,3,64,4,512]{4,3,2,1,0:T(4,128)(2,1)} %bitcast.28, bf16[4,20,1152]{2,1,0:T(8,128)(2,1)} %bitcast.30, bf16[4,20,1152]{2,1,0:T(8,128)(2,1)} %bitcast.32), custom_call_target="tpu_custom_call" | custom-call | bytes 6291456 | tf_op jit(solution)/shard_map/input_weights/pallas_call | solution.py:43
  24.7 0.0 copy-done.5
  24.7 0.1 collective-permute-start.2
  24.8 0.0 copy-done.6
  24.8 2.0 %collective-permute-start.4 = (bf16[2,36,1152]{2,1,0:T(8,128)(2,1)S(1)}, bf16[2,36,1152]{2,1,0:T(8,128)(2,1)S(1)}, u32[]{:S(2)}, u32[]{:S(2)}) collective-permute-start(bf16[2,36,1152]{2,1,0:T(8,128)(2,1)S(1)} %collective-permute-done.3.refs_3_.refs_8_.refs_11_.refs_4_), channel_id=1, source_target_pairs={{0,1},{1,0},{2,3},{3,2},{4,5},{5,4},{6,7},{7,6},{8,9},{9,8},{10,11... | collective-permute-start | bytes 497672 | tf_op jit(solution)/shard_map/ppermute | solution.py:404
  26.7 0.0 collective-permute-done.7.refs_5_.refs_10_.refs_13_.refs_6_
  26.7 0.0 copy-start.1
  26.7 0.1 collective-permute-start.8
  26.8 0.0 collective-permute-done.5.refs_4_.refs_9_.refs_12_.refs_5_
  26.8 0.0 copy-start.2
  26.8 2.0 %collective-permute-start.6 = (bf16[4,20,1152]{2,1,0:T(8,128)(2,1)S(1)}, bf16[4,20,1152]{2,1,0:T(8,128)(2,1)S(1)}, u32[]{:S(2)}, u32[]{:S(2)}) collective-permute-start(bf16[4,20,1152]{2,1,0:T(8,128)(2,1)S(1)} %collective-permute-done.5.refs_4_.refs_9_.refs_12_.refs_5_), channel_id=1, source_target_pairs={{0,1},{1,0},{2,3},{3,2},{4,5},{5,4},{6,7},{7,6},{8,9},{9,8},{10,11... | collective-permute-start | bytes 552968 | tf_op jit(solution)/shard_map/ppermute | solution.py:404
  28.8 0.0 copy-done.1
  28.8 0.0 copy-done.2
  28.8 44.5 %step0.2 = (f32[4,2,768,512]{3,2,1,0:T(8,128)}, bf16[4,2,2,3,1024,512]{5,4,3,2,1,0:T(8,128)(2,1)}) custom-call(s32[6]{0:T(128)} %stack.63.refs_0_, bf16[36,36,512]{2,1,0:T(8,128)(2,1)} %refs_1_.1, bf16[2,36,1152]{2,1,0:T(8,128)(2,1)} %copy-done.5, bf16[2,36,1152]{2,1,0:T(8,128)(2,1)} %copy-done.6, bf16[4,20,1152]{2,1,0:T(8,128)(2,1)} %copy-done.2, ...), custom_call_target="tpu_custom_call" | custom-call | flops 19327352832 | bytes 25165824 | tf_op jit(solution)/shard_map/step0/pallas_call | solution.py:372
  73.3 0.0 collective-permute-done.2.refs_2_
  73.3 0.0 copy-start.9
  73.3 0.0 collective-permute-done.4.refs_3_
  73.3 0.0 copy-start.10
  73.3 0.0 collective-permute-done.8.refs_5_
  73.3 0.0 copy-start.7
  73.3 0.0 collective-permute-done.6.refs_4_
  73.4 0.0 copy-start.8
  73.4 0.0 collective-permute-done.refs_1_
  73.4 0.0 copy-start
  73.4 0.6 copy-done.9
  74.0 0.1 copy-done.10
  74.0 0.1 copy-done.7
  74.1 0.1 copy-done.8
  74.2 0.5 copy-done
  74.7 43.1 %step0.3 = (bf16[2,768,512]{2,1,0:T(8,128)(2,1)}, f32[4,2,768,128]{3,2,1,0:T(8,128)}, bf16[4,2,2,3,1024,512]{5,4,3,2,1,0:T(8,128)(2,1)}) custom-call(s32[6]{0:T(128)} %stack.63.refs_0_, bf16[36,36,512]{2,1,0:T(8,128)(2,1)} %copy-done, bf16[2,36,1152]{2,1,0:T(8,128)(2,1)} %copy-done.9, ...), custom_call_target="tpu_custom_call", output_to_operand_aliasing={{2}: (8, {})} | custom-call | flops 19327352832 | bytes 25165824 | tf_op jit(solution)/shard_map/step0/pallas_call | solution.py:372
  117.7 0.5 collective-permute-start.9
  118.3 32.0 %step1.2.refs_2_ = f32[4,2,720,512]{3,2,1,0:T(8,128)} custom-call(s32[6]{0:T(128)} %stack.63.refs_0_, bf16[2,768,512]{2,1,0:T(8,128)(2,1)} %get-tuple-element.9.refs_1_, bf16[36,36,128]{2,1,0:T(8,128)(2,1)} %refs_2_.1, bf16[2,36,1152]{2,1,0:T(8,128)(2,1)} %copy-done.5, bf16[2,36,1152]{2,1,0:T(8,128)(2,1)} %copy-done.6, bf16[4,20,1152]{2,1,0:T(8,128)(2,1)} %copy-done.2, ...), custom_call_target="tpu_custom_call" | custom-call | flops 18119393280 | bytes 25165824 | tf_op jit(solution)/shard_map/step1/pallas_call | solution.py:372
  150.3 4.4 %collective-permute-done.9.refs_1_ = bf16[2,768,512]{2,1,0:T(8,128)(2,1)S(1)} collective-permute-done((bf16[2,768,512]{2,1,0:T(8,128)(2,1)}, bf16[2,768,512]{2,1,0:T(8,128)(2,1)S(1)}, u32[]{:S(2)}, u32[]{:S(2)}) %collective-permute-start.9) | collective-permute-done | bytes 1572896 | tf_op jit(solution)/shard_map/ppermute | solution.py:404
  154.7 0.0 copy-start.11
  154.7 1.2 copy-done.11
  155.8 27.9 %step1.3 = (bf16[36,36,512]{2,1,0:T(8,128)(2,1)}, f32[36,36,512]{2,1,0:T(8,128)}) custom-call(s32[6]{0:T(128)} %stack.63.refs_0_, bf16[2,768,512]{2,1,0:T(8,128)(2,1)} %copy-done.11, f32[4,2,720,512]{3,2,1,0:T(8,128)} %step1.2.refs_2_, bf16[4,2,2,3,1024,512]{5,4,3,2,1,0:T(8,128)(2,1)} %get-tuple-element.10.refs_9_.refs_3_, ...), custom_call_target="tpu_custom_call" | custom-call | flops 18119393280 | bytes 25165824 | tf_op jit(solution)/shard_map/step1/pallas_call | solution.py:372
  (23 shorter events, 0.3 us)
Async XLA Ops:
  3.3 7.3 %collective-permute-start.1 = (bf16[2,36,1152]{2,1,0:T(8,128)(2,1)S(1)}, bf16[2,36,1152]{2,1,0:T(8,128)(2,1)S(1)}, u32[]{:S(2)}, u32[]{:S(2)}) collective-permute-start(bf16[2,36,1152]{2,1,0:T(8,128)(2,1)S(1)} %maximum_maximum_fusion), channel_id=1, source_target_pairs={{0,8},{8,16},{16,24},{1,9},{9,17},{17,25},{2,10},{10,18},{18,26},{... | collective-permute-start | bytes 497672 | tf_op jit(solution)/shard_map/ppermute | solution.py:395
  5.7 5.4 %collective-permute-start.3 = (bf16[2,36,1152]{2,1,0:T(8,128)(2,1)S(1)}, bf16[2,36,1152]{2,1,0:T(8,128)(2,1)S(1)}, u32[]{:S(2)}, u32[]{:S(2)}) collective-permute-start(bf16[2,36,1152]{2,1,0:T(8,128)(2,1)S(1)} %maximum_maximum_fusion.1), channel_id=1, source_target_pairs={{8,0},{16,8},{24,16},{9,1},{17,9},{25,17},{10,2},{18,10},{26,18},{... | collective-permute-start | bytes 497672 | tf_op jit(solution)/shard_map/ppermute | solution.py:400
  10.6 14.1 %copy-start.5 = (bf16[2,36,1152]{2,1,0:T(8,128)(2,1)}, bf16[2,36,1152]{2,1,0:T(8,128)(2,1)S(1)}, u32[]{:S(2)}) copy-start(bf16[2,36,1152]{2,1,0:T(8,128)(2,1)S(1)} %collective-permute-done.1.refs_2_.refs_7_.refs_10_.refs_3_) | copy-start | bytes 497668
  11.1 13.7 %copy-start.6 = (bf16[2,36,1152]{2,1,0:T(8,128)(2,1)}, bf16[2,36,1152]{2,1,0:T(8,128)(2,1)S(1)}, u32[]{:S(2)}) copy-start(bf16[2,36,1152]{2,1,0:T(8,128)(2,1)S(1)} %collective-permute-done.3.refs_3_.refs_8_.refs_11_.refs_4_) | copy-start | bytes 497668
  11.6 8.6 %copy-start.3 = (bf16[20,2,2,1152]{3,0,1,2:T(8,128)(2,1)}, bf16[20,2,2,1152]{3,0,1,2:T(8,128)(2,1)S(1)}, u32[]{:S(2)}) copy-start(bf16[20,2,2,1152]{3,0,1,2:T(8,128)(2,1)S(1)} %copy.18) | copy-start | bytes 552964
  11.6 8.5 %copy-start.4 = (bf16[20,2,2,1152]{3,0,1,2:T(8,128)(2,1)}, bf16[20,2,2,1152]{3,0,1,2:T(8,128)(2,1)S(1)}, u32[]{:S(2)}) copy-start(bf16[20,2,2,1152]{3,0,1,2:T(8,128)(2,1)S(1)} %copy.24) | copy-start | bytes 552964
  11.7 15.1 %collective-permute-start.7 = (bf16[4,20,1152]{2,1,0:T(8,128)(2,1)S(1)}, bf16[4,20,1152]{2,1,0:T(8,128)(2,1)S(1)}, u32[]{:S(2)}, u32[]{:S(2)}) collective-permute-start(bf16[4,20,1152]{2,1,0:T(8,128)(2,1)S(1)} %bitcast.31), channel_id=1, source_target_pairs={{2,0},{4,2},{6,4},{3,1},{5,3},{7,5},{10,8},{12,10},{14,12},{11,9},... | collective-permute-start | bytes 552968 | tf_op jit(solution)/shard_map/ppermute | solution.py:400
  13.0 13.9 %collective-permute-start.5 = (bf16[4,20,1152]{2,1,0:T(8,128)(2,1)S(1)}, bf16[4,20,1152]{2,1,0:T(8,128)(2,1)S(1)}, u32[]{:S(2)}, u32[]{:S(2)}) collective-permute-start(bf16[4,20,1152]{2,1,0:T(8,128)(2,1)S(1)} %bitcast.29), channel_id=1, source_target_pairs={{0,2},{2,4},{4,6},{1,3},{3,5},{5,7},{8,10},{10,12},{12,14},{9,11},... | collective-permute-start | bytes 552968 | tf_op jit(solution)/shard_map/ppermute | solution.py:395
  17.6 55.8 %collective-permute-start = (bf16[36,36,512]{2,1,0:T(8,128)(2,1)}, bf16[36,36,512]{2,1,0:T(8,128)(2,1)S(1)}, u32[]{:S(2)}, u32[]{:S(2)}) collective-permute-start(bf16[36,36,512]{2,1,0:T(8,128)(2,1)} %refs_1_.1), channel_id=1, source_target_pairs={{0,1},{1,0},{2,3},{3,2},{4,5},{5,4},{6,7},{7,6},{8,9},{9,8},{10,11... | collective-permute-start | bytes 3981320 | tf_op jit(solution)/shard_map/ppermute | solution.py:404
  24.7 48.6 %collective-permute-start.2 = (bf16[2,36,1152]{2,1,0:T(8,128)(2,1)S(1)}, bf16[2,36,1152]{2,1,0:T(8,128)(2,1)S(1)}, u32[]{:S(2)}, u32[]{:S(2)}) collective-permute-start(bf16[2,36,1152]{2,1,0:T(8,128)(2,1)S(1)} %collective-permute-done.1.refs_2_.refs_7_.refs_10_.refs_3_), channel_id=1, source_target_pairs={{0,1},{1,0},{2,3},{3,2},{4,5},{5,4},{6,7},{7,6},{8,9},{9,8},{10,11... | collective-permute-start | bytes 497672 | tf_op jit(solution)/shard_map/ppermute | solution.py:404
  24.8 48.5 %collective-permute-start.4 = (bf16[2,36,1152]{2,1,0:T(8,128)(2,1)S(1)}, bf16[2,36,1152]{2,1,0:T(8,128)(2,1)S(1)}, u32[]{:S(2)}, u32[]{:S(2)}) collective-permute-start(bf16[2,36,1152]{2,1,0:T(8,128)(2,1)S(1)} %collective-permute-done.3.refs_3_.refs_8_.refs_11_.refs_4_), channel_id=1, source_target_pairs={{0,1},{1,0},{2,3},{3,2},{4,5},{5,4},{6,7},{7,6},{8,9},{9,8},{10,11... | collective-permute-start | bytes 497672 | tf_op jit(solution)/shard_map/ppermute | solution.py:404
  26.7 2.1 %copy-start.1 = (bf16[4,20,1152]{2,1,0:T(8,128)(2,1)}, bf16[4,20,1152]{2,1,0:T(8,128)(2,1)S(1)}, u32[]{:S(2)}) copy-start(bf16[4,20,1152]{2,1,0:T(8,128)(2,1)S(1)} %collective-permute-done.7.refs_5_.refs_10_.refs_13_.refs_6_) | copy-start | bytes 552964
  26.7 46.6 %collective-permute-start.8 = (bf16[4,20,1152]{2,1,0:T(8,128)(2,1)S(1)}, bf16[4,20,1152]{2,1,0:T(8,128)(2,1)S(1)}, u32[]{:S(2)}, u32[]{:S(2)}) collective-permute-start(bf16[4,20,1152]{2,1,0:T(8,128)(2,1)S(1)} %collective-permute-done.7.refs_5_.refs_10_.refs_13_.refs_6_), channel_id=1, source_target_pairs={{0,1},{1,0},{2,3},{3,2},{4,5},{5,4},{6,7},{7,6},{8,9},{9,8},{10,11... | collective-permute-start | bytes 552968 | tf_op jit(solution)/shard_map/ppermute | solution.py:404
  26.8 2.0 %copy-start.2 = (bf16[4,20,1152]{2,1,0:T(8,128)(2,1)}, bf16[4,20,1152]{2,1,0:T(8,128)(2,1)S(1)}, u32[]{:S(2)}) copy-start(bf16[4,20,1152]{2,1,0:T(8,128)(2,1)S(1)} %collective-permute-done.5.refs_4_.refs_9_.refs_12_.refs_5_) | copy-start | bytes 552964
  26.8 46.5 %collective-permute-start.6 = (bf16[4,20,1152]{2,1,0:T(8,128)(2,1)S(1)}, bf16[4,20,1152]{2,1,0:T(8,128)(2,1)S(1)}, u32[]{:S(2)}, u32[]{:S(2)}) collective-permute-start(bf16[4,20,1152]{2,1,0:T(8,128)(2,1)S(1)} %collective-permute-done.5.refs_4_.refs_9_.refs_12_.refs_5_), channel_id=1, source_target_pairs={{0,1},{1,0},{2,3},{3,2},{4,5},{5,4},{6,7},{7,6},{8,9},{9,8},{10,11... | collective-permute-start | bytes 552968 | tf_op jit(solution)/shard_map/ppermute | solution.py:404
  73.3 0.7 copy-start.9
  73.3 0.7 copy-start.10
  73.3 0.8 copy-start.7
  73.4 0.8 copy-start.8
  73.4 1.3 copy-start
  117.7 36.9 %collective-permute-start.9 = (bf16[2,768,512]{2,1,0:T(8,128)(2,1)}, bf16[2,768,512]{2,1,0:T(8,128)(2,1)S(1)}, u32[]{:S(2)}, u32[]{:S(2)}) collective-permute-start(bf16[2,768,512]{2,1,0:T(8,128)(2,1)} %get-tuple-element.9.refs_1_), channel_id=1, source_target_pairs={{0,1},{1,0},{2,3},{3,2},{4,5},{5,4},{6,7},{7,6},{8,9},{9,8},{10,11... | collective-permute-start | bytes 4718600 | tf_op jit(solution)/shard_map/ppermute | solution.py:404
  154.7 1.2 copy-start.11

commit v4 on v3

--- a/solution.py
+++ b/solution.py
@@ -84,7 +84,7 @@
 
 
 def pass_kernel(dims, *refs):
-    sizes, height, tiles, step, raw, first, final, into = dims
+    sizes, height, tiles, step, raw, first, final, into, which = dims
     rows, cols, stride = sizes
     fused = step == 0
     key_ref, refs = refs[0], list(refs[1:])
@@ -108,16 +108,14 @@
     else:
         (pre_ref,) = take(1)
     if fused:
-        (u_ref,) = take(1)
+        (made_ref,) = take(1)
     v_ref, wide_ref = take(2)
     if first:
         (x_ref,) = take(1)
-    if final:
-        (pre_ref,) = take(1)
     if final and step == 0:
         cell_ref, mask_ref = take(2)
     if fused:
-        (flat_ref,) = take(1)
+        flat_ref, u_ref, copied = take(3)
     channels = v_ref.shape[2] // 3
 
     def surrounded(tile_refs, lanes):
@@ -244,46 +242,50 @@
                 cell_out[2 * t + p] = cell[r]
                 hidden_out[2 * t + p] = hidden[r].astype(BF16)
 
-    chunk = 32
-    groups = 3 if fused else 1
-    depth = 3 * channels // groups
-    if fused:
-        for c in range(0, channels, chunk):
-            transform(0, c, chunk)
-    for group in range(groups):
-        ready = group * depth
-        waiting = []
-        if fused and group < 2:
-            waiting = [(group + 1, c, chunk) for c in range(0, channels, chunk)]
-        share = -(-len(waiting) // (4 * len(tiles)))
-        for low, high in tiles:
-            m = slice(low, high)
-            made = {}
-            for k in (1, 2, 0, 3):
-                place_of = {1: (0, 0), 2: (0, 1), 0: (1, 0), 3: (1, 1)}[k]
-                if fused:
-                    weights = u_ref[0, place_of[0], place_of[1], group]
-                else:
-                    weights = u_ref[0, place_of[0], place_of[1]].reshape(depth, GATES)
-                made[k] = dot(v_ref[k, m, ready : ready + depth], weights)
-                for _ in range(share):
-                    if waiting:
-                        transform(*waiting.pop(0))
-            for p in range(2):
-                if group > 0:
-                    other = pre_ref[0, p, m, :]
-                elif first:
-                    bias = jnp.concatenate([bias_ref[k : k + 1, :] for k in range(4)], axis=1)
-                    other = dot(x_ref[p, m, :], w_ref[0]) + bias
-                else:
-                    other = before_ref[0, p, m, :]
-                both = made[1] - made[2] if p else made[1] + made[2]
-                edge = -made[3] if p else made[0]
-                pre = 0.5 * both + edge + other
-                if final and group == groups - 1:
-                    gates(low, high, p, pre)
-                else:
-                    pre_ref[0, p, m, :] = pre
+    n = pl.program_id(0)
+
+    def leave(block, b):
+        half = pl.ds(pl.multiple_of(key_ref[which] * channels, channels), channels)
+        return pltpu.make_async_copy(
+            u_ref.at[0, :, :, b], made_ref.at[block, :, :, b, half, :], copied.at[b]
+        )
+
+    if fused:
+        chunk = 32
+        for b in range(3):
+
+            @pl.when(n > 0)
+            def _(b=b):
+                leave(n - 1, b).wait()
+
+            for c in range(0, channels, chunk):
+                transform(b, c, chunk)
+            leave(n, b).start()
+    depth = 3 * channels
+    for low, high in tiles:
+        m = slice(low, high)
+        made = {}
+        for k, s, t in ((1, 0, 0), (2, 0, 1), (0, 1, 0), (3, 1, 1)):
+            made[k] = dot(v_ref[k, m, :], u_ref[0, s, t].reshape(depth, GATES))
+        for p in range(2):
+            if first:
+                bias = jnp.concatenate([bias_ref[k : k + 1, :] for k in range(4)], axis=1)
+                other = dot(x_ref[p, m, :], w_ref[0]) + bias
+            else:
+                other = before_ref[0, p, m, :]
+            both = made[1] - made[2] if p else made[1] + made[2]
+            edge = -made[3] if p else made[0]
+            pre = 0.5 * both + edge + other
+            if final:
+                gates(low, high, p, pre)
+            else:
+                pre_ref[0, p, m, :] = pre
+    if fused:
+
+        @pl.when(n == pl.num_programs(0) - 1)
+        def _():
+            for b in range(3):
+                leave(n, b).wait()
 
 
 def run_pass(step, sizes, key, which, hidden, u, frame=None, before=None, cell=None, into=None):
@@ -298,7 +300,7 @@
     middle = up_to(height // 2, 2 * stride if step else 16)
     tiles = ((0, middle), (middle, height))
     wide = up_to(max((rows // 2 + 2) * stride, height + stride + 2), 8)
-    dims = (sizes, height, tiles, step, raw, first, final, int(into is not None))
+    dims = (sizes, height, tiles, step, raw, first, final, int(into is not None), which)
     once = pl.Buffered(1)
 
     def whole(array):
@@ -343,13 +345,13 @@
     ]
     if first:
         scratch.append(pltpu.VMEM((2, height, 6 * LANES), BF16))
-    if final:
-        scratch.append(pltpu.VMEM((1, 2, height, GATES), F32))
     if final and step == 0:
         scratch.append(pltpu.VMEM((1, 2, height, LANES), F32))
         scratch.append(pltpu.VMEM((2, height, LANES), F32))
     if fused:
         scratch.append(pltpu.VMEM((3, 4 * channels, LANES), F32))
+        scratch.append(pltpu.VMEM((1, 2, 2, 3, channels, GATES), BF16))
+        scratch.append(pltpu.SemaphoreType.DMA((3,)))
     if not final:
         out_specs = [pl.BlockSpec((1, 2, height, GATES), lambda n, k: (n, 0, 0, 0))]
         out_shape = [jax.ShapeDtypeStruct((count, 2, height, GATES), F32)]
@@ -367,7 +369,7 @@
         out_specs = [pl.BlockSpec((rows, cols, LANES), lambda n, k: (0, 0, n))] * 2
         out_shape = [jax.ShapeDtypeStruct(shape, BF16), jax.ShapeDtypeStruct(shape, F32)]
     if fused:
-        out_specs.append(u_spec)
+        out_specs.append(pl.BlockSpec(memory_space=pl.ANY))
         out_shape.append(jax.ShapeDtypeStruct((count, 2, 2, 3, 2 * channels, GATES), BF16))
     return pl.pallas_call(
         functools.partial(pass_kernel, dims),

time: 184 us -> 176 us (0.957)
  Pallas kernels: 152 us -> 144 us
    pallas_call x4, Pallas kernels: 147 us -> 139 us  [run_pass(): pl.pallas_call(functools.partial(pass_kernel, dims), grid_spec=pltpu.Pref...]
where the time goes in v4:
time: 176 us
  Pallas kernels  144 us (82%)
  starting transfers between devices  16.3 us (9%)
  local copies, waits for them, and re-layouts  8.59 us (5%)
  waiting for transfers between devices  5 us (3%)
    pallas_call x4, Pallas kernels, run_pass(): pl.pallas_call(functools.partial(pass_kernel, dims), grid_spec=pltpu.Pref...  139 us
    ppermute x2, starting transfers between devices, forward(): return lax.ppermute(x, axis, [(i, i + 1) for i in range(count - 1)])  6.99 us
    ppermute x6, starting transfers between devices, swapped(): return lax.ppermute(x, 'ch', [(0, 1), (1, 0)])  6.71 us
    ppermute x6, waiting for transfers between devices, swapped(): return lax.ppermute(x, 'ch', [(0, 1), (1, 0)])  4.64 us
    pallas_call x1, Pallas kernels, input_weights(): pl.pallas_call(functools.partial(input_weights_kernel, depth, blocks), gr...  4.53 us
  transfers between devices with their start and end apart: 10, of which 2 were waited for; matrix products, arithmetic and copies ran while one was open for 2% of the time, Pallas kernels for 44%

profile of v4, /device:TPU:0, one launch (start us, length us, event | category | flops | bytes accessed | tf_op | source)
XLA Modules:
  0.0 175.9 jit_solution(2040589551931219050)
XLA Ops:
  0.6 0.8 fusion.16
  1.4 0.9 reduce-precision_convert_fusion.2
  2.3 0.9 fusion.14
  3.3 2.4 %collective-permute-start.1 = (bf16[2,36,1152]{2,1,0:T(8,128)(2,1)S(1)}, bf16[2,36,1152]{2,1,0:T(8,128)(2,1)S(1)}, u32[]{:S(2)}, u32[]{:S(2)}) collective-permute-start(bf16[2,36,1152]{2,1,0:T(8,128)(2,1)S(1)} %maximum_maximum_fusion), channel_id=1, source_target_pairs={{0,8},{8,16},{16,24},{1,9},{9,17},{17,25},{2,10},{10,18},{18,26},{... | collective-permute-start | bytes 497672 | tf_op jit(solution)/shard_map/ppermute | solution.py:397
  5.7 1.3 collective-permute-start.3
  7.0 1.0 fusion.15
  8.0 1.4 fusion.12
  9.3 1.2 fusion.13
  10.6 0.0 collective-permute-done.1.refs_2_.refs_7_.refs_10_.refs_3_
  10.6 0.0 copy-start.5
  10.8 0.4 collective-permute-done.3.refs_3_.refs_8_.refs_11_.refs_4_
  11.1 0.0 copy-start.6
  11.2 0.1 pad_maximum_fusion.1
  11.3 0.1 reshape.24
  11.4 0.1 pad_maximum_fusion
  11.5 0.1 reshape.22
  11.6 0.0 copy-start.3
  11.6 0.0 copy-start.4
  11.7 1.3 collective-permute-start.7
  13.0 4.6 %collective-permute-start.5 = (bf16[4,20,1152]{2,1,0:T(8,128)(2,1)S(1)}, bf16[4,20,1152]{2,1,0:T(8,128)(2,1)S(1)}, u32[]{:S(2)}, u32[]{:S(2)}) collective-permute-start(bf16[4,20,1152]{2,1,0:T(8,128)(2,1)S(1)} %bitcast.29), channel_id=1, source_target_pairs={{0,2},{2,4},{4,6},{1,3},{3,5},{5,7},{8,10},{10,12},{12,14},{9,11},... | collective-permute-start | bytes 552968 | tf_op jit(solution)/shard_map/ppermute | solution.py:397
  17.6 2.0 %collective-permute-start = (bf16[36,36,512]{2,1,0:T(8,128)(2,1)}, bf16[36,36,512]{2,1,0:T(8,128)(2,1)S(1)}, u32[]{:S(2)}, u32[]{:S(2)}) collective-permute-start(bf16[36,36,512]{2,1,0:T(8,128)(2,1)} %refs_1_.1), channel_id=1, source_target_pairs={{0,1},{1,0},{2,3},{3,2},{4,5},{5,4},{6,7},{7,6},{8,9},{9,8},{10,11... | collective-permute-start | bytes 3981320 | tf_op jit(solution)/shard_map/ppermute | solution.py:406
  19.6 0.6 stack.63.refs_0_
  20.2 0.0 copy-done.3
  20.2 0.0 copy-done.4
  20.2 4.5 %input_weights.1.refs_11_.refs_7_ = bf16[4,768,512]{2,1,0:T(8,128)(2,1)} custom-call(bf16[3,3,64,4,512]{4,3,2,1,0:T(4,128)(2,1)} %bitcast.28, bf16[4,20,1152]{2,1,0:T(8,128)(2,1)} %bitcast.30, bf16[4,20,1152]{2,1,0:T(8,128)(2,1)} %bitcast.32), custom_call_target="tpu_custom_call" | custom-call | bytes 6291456 | tf_op jit(solution)/shard_map/input_weights/pallas_call | solution.py:43
  24.7 0.0 copy-done.5
  24.7 0.1 collective-permute-start.2
  24.8 0.0 copy-done.6
  24.8 2.0 %collective-permute-start.4 = (bf16[2,36,1152]{2,1,0:T(8,128)(2,1)S(1)}, bf16[2,36,1152]{2,1,0:T(8,128)(2,1)S(1)}, u32[]{:S(2)}, u32[]{:S(2)}) collective-permute-start(bf16[2,36,1152]{2,1,0:T(8,128)(2,1)S(1)} %collective-permute-done.3.refs_3_.refs_8_.refs_11_.refs_4_), channel_id=1, source_target_pairs={{0,1},{1,0},{2,3},{3,2},{4,5},{5,4},{6,7},{7,6},{8,9},{9,8},{10,11... | collective-permute-start | bytes 497672 | tf_op jit(solution)/shard_map/ppermute | solution.py:406
  26.7 0.0 collective-permute-done.7.refs_5_.refs_10_.refs_13_.refs_6_
  26.7 0.0 copy-start.1
  26.7 0.1 collective-permute-start.8
  26.8 0.0 collective-permute-done.5.refs_4_.refs_9_.refs_12_.refs_5_
  26.8 0.0 copy-start.2
  26.8 2.0 %collective-permute-start.6 = (bf16[4,20,1152]{2,1,0:T(8,128)(2,1)S(1)}, bf16[4,20,1152]{2,1,0:T(8,128)(2,1)S(1)}, u32[]{:S(2)}, u32[]{:S(2)}) collective-permute-start(bf16[4,20,1152]{2,1,0:T(8,128)(2,1)S(1)} %collective-permute-done.5.refs_4_.refs_9_.refs_12_.refs_5_), channel_id=1, source_target_pairs={{0,1},{1,0},{2,3},{3,2},{4,5},{5,4},{6,7},{7,6},{8,9},{9,8},{10,11... | collective-permute-start | bytes 552968 | tf_op jit(solution)/shard_map/ppermute | solution.py:406
  28.8 0.0 copy-done.1
  28.8 0.0 copy-done.2
  28.8 41.6 %step0.2 = (f32[4,2,768,512]{3,2,1,0:T(8,128)}, bf16[4,2,2,3,1024,512]{5,4,3,2,1,0:T(8,128)(2,1)}) custom-call(s32[6]{0:T(128)} %stack.63.refs_0_, bf16[36,36,512]{2,1,0:T(8,128)(2,1)} %refs_1_.1, bf16[2,36,1152]{2,1,0:T(8,128)(2,1)} %copy-done.5, bf16[2,36,1152]{2,1,0:T(8,128)(2,1)} %copy-done.6, bf16[4,20,1152]{2,1,0:T(8,128)(2,1)} %copy-done.2, ...), custom_call_target="tpu_custom_call" | custom-call | flops 19327352832 | bytes 25165824 | tf_op jit(solution)/shard_map/step0/pallas_call | solution.py:374
  70.4 0.0 collective-permute-done.2.refs_2_
  70.4 0.0 copy-start.9
  70.4 0.0 collective-permute-done.4.refs_3_
  70.4 0.0 copy-start.10
  70.4 0.0 collective-permute-done.8.refs_5_
  70.4 0.0 copy-start.7
  70.5 0.0 collective-permute-done.6.refs_4_
  70.5 0.0 copy-start.8
  70.5 0.0 collective-permute-done.refs_1_
  70.5 0.0 copy-start
  70.5 0.6 copy-done.9
  71.1 0.1 copy-done.10
  71.2 0.1 copy-done.7
  71.2 0.1 copy-done.8
  71.3 0.5 copy-done
  71.8 37.8 %step0.3 = (bf16[2,768,512]{2,1,0:T(8,128)(2,1)}, f32[4,2,768,128]{3,2,1,0:T(8,128)}, bf16[4,2,2,3,1024,512]{5,4,3,2,1,0:T(8,128)(2,1)}) custom-call(s32[6]{0:T(128)} %stack.63.refs_0_, bf16[36,36,512]{2,1,0:T(8,128)(2,1)} %copy-done, bf16[2,36,1152]{2,1,0:T(8,128)(2,1)} %copy-done.9, ...), custom_call_target="tpu_custom_call", output_to_operand_aliasing={{2}: (8, {})} | custom-call | flops 19327352832 | bytes 25165824 | tf_op jit(solution)/shard_map/step0/pallas_call | solution.py:374
  109.6 0.6 collective-permute-start.9
  110.2 31.8 %step1.2.refs_2_ = f32[4,2,720,512]{3,2,1,0:T(8,128)} custom-call(s32[6]{0:T(128)} %stack.63.refs_0_, bf16[2,768,512]{2,1,0:T(8,128)(2,1)} %get-tuple-element.9.refs_1_, bf16[36,36,128]{2,1,0:T(8,128)(2,1)} %refs_2_.1, bf16[2,36,1152]{2,1,0:T(8,128)(2,1)} %copy-done.5, bf16[2,36,1152]{2,1,0:T(8,128)(2,1)} %copy-done.6, bf16[4,20,1152]{2,1,0:T(8,128)(2,1)} %copy-done.2, ...), custom_call_target="tpu_custom_call" | custom-call | flops 18119393280 | bytes 25165824 | tf_op jit(solution)/shard_map/step1/pallas_call | solution.py:374
  142.0 4.6 %collective-permute-done.9.refs_1_ = bf16[2,768,512]{2,1,0:T(8,128)(2,1)S(1)} collective-permute-done((bf16[2,768,512]{2,1,0:T(8,128)(2,1)}, bf16[2,768,512]{2,1,0:T(8,128)(2,1)S(1)}, u32[]{:S(2)}, u32[]{:S(2)}) %collective-permute-start.9) | collective-permute-done | bytes 1572896 | tf_op jit(solution)/shard_map/ppermute | solution.py:406
  146.6 0.0 copy-start.11
  146.6 1.2 copy-done.11
  147.8 28.2 %step1.3 = (bf16[36,36,512]{2,1,0:T(8,128)(2,1)}, f32[36,36,512]{2,1,0:T(8,128)}) custom-call(s32[6]{0:T(128)} %stack.63.refs_0_, bf16[2,768,512]{2,1,0:T(8,128)(2,1)} %copy-done.11, f32[4,2,720,512]{3,2,1,0:T(8,128)} %step1.2.refs_2_, bf16[4,2,2,3,1024,512]{5,4,3,2,1,0:T(8,128)(2,1)} %get-tuple-element.10.refs_9_.refs_3_, ...), custom_call_target="tpu_custom_call" | custom-call | flops 18119393280 | bytes 25165824 | tf_op jit(solution)/shard_map/step1/pallas_call | solution.py:374
  (23 shorter events, 0.3 us)
Async XLA Ops:
  3.3 7.3 %collective-permute-start.1 = (bf16[2,36,1152]{2,1,0:T(8,128)(2,1)S(1)}, bf16[2,36,1152]{2,1,0:T(8,128)(2,1)S(1)}, u32[]{:S(2)}, u32[]{:S(2)}) collective-permute-start(bf16[2,36,1152]{2,1,0:T(8,128)(2,1)S(1)} %maximum_maximum_fusion), channel_id=1, source_target_pairs={{0,8},{8,16},{16,24},{1,9},{9,17},{17,25},{2,10},{10,18},{18,26},{... | collective-permute-start | bytes 497672 | tf_op jit(solution)/shard_map/ppermute | solution.py:397
  5.7 5.4 %collective-permute-start.3 = (bf16[2,36,1152]{2,1,0:T(8,128)(2,1)S(1)}, bf16[2,36,1152]{2,1,0:T(8,128)(2,1)S(1)}, u32[]{:S(2)}, u32[]{:S(2)}) collective-permute-start(bf16[2,36,1152]{2,1,0:T(8,128)(2,1)S(1)} %maximum_maximum_fusion.1), channel_id=1, source_target_pairs={{8,0},{16,8},{24,16},{9,1},{17,9},{25,17},{10,2},{18,10},{26,18},{... | collective-permute-start | bytes 497672 | tf_op jit(solution)/shard_map/ppermute | solution.py:402
  10.6 14.1 %copy-start.5 = (bf16[2,36,1152]{2,1,0:T(8,128)(2,1)}, bf16[2,36,1152]{2,1,0:T(8,128)(2,1)S(1)}, u32[]{:S(2)}) copy-start(bf16[2,36,1152]{2,1,0:T(8,128)(2,1)S(1)} %collective-permute-done.1.refs_2_.refs_7_.refs_10_.refs_3_) | copy-start | bytes 497668
  11.1 13.7 %copy-start.6 = (bf16[2,36,1152]{2,1,0:T(8,128)(2,1)}, bf16[2,36,1152]{2,1,0:T(8,128)(2,1)S(1)}, u32[]{:S(2)}) copy-start(bf16[2,36,1152]{2,1,0:T(8,128)(2,1)S(1)} %collective-permute-done.3.refs_3_.refs_8_.refs_11_.refs_4_) | copy-start | bytes 497668
  11.6 8.6 %copy-start.3 = (bf16[20,2,2,1152]{3,0,1,2:T(8,128)(2,1)}, bf16[20,2,2,1152]{3,0,1,2:T(8,128)(2,1)S(1)}, u32[]{:S(2)}) copy-start(bf16[20,2,2,1152]{3,0,1,2:T(8,128)(2,1)S(1)} %copy.18) | copy-start | bytes 552964
  11.6 8.5 %copy-start.4 = (bf16[20,2,2,1152]{3,0,1,2:T(8,128)(2,1)}, bf16[20,2,2,1152]{3,0,1,2:T(8,128)(2,1)S(1)}, u32[]{:S(2)}) copy-start(bf16[20,2,2,1152]{3,0,1,2:T(8,128)(2,1)S(1)} %copy.24) | copy-start | bytes 552964
  11.7 15.1 %collective-permute-start.7 = (bf16[4,20,1152]{2,1,0:T(8,128)(2,1)S(1)}, bf16[4,20,1152]{2,1,0:T(8,128)(2,1)S(1)}, u32[]{:S(2)}, u32[]{:S(2)}) collective-permute-start(bf16[4,20,1152]{2,1,0:T(8,128)(2,1)S(1)} %bitcast.31), channel_id=1, source_target_pairs={{2,0},{4,2},{6,4},{3,1},{5,3},{7,5},{10,8},{12,10},{14,12},{11,9},... | collective-permute-start | bytes 552968 | tf_op jit(solution)/shard_map/ppermute | solution.py:402
  13.0 13.9 %collective-permute-start.5 = (bf16[4,20,1152]{2,1,0:T(8,128)(2,1)S(1)}, bf16[4,20,1152]{2,1,0:T(8,128)(2,1)S(1)}, u32[]{:S(2)}, u32[]{:S(2)}) collective-permute-start(bf16[4,20,1152]{2,1,0:T(8,128)(2,1)S(1)} %bitcast.29), channel_id=1, source_target_pairs={{0,2},{2,4},{4,6},{1,3},{3,5},{5,7},{8,10},{10,12},{12,14},{9,11},... | collective-permute-start | bytes 552968 | tf_op jit(solution)/shard_map/ppermute | solution.py:397
  17.6 52.9 %collective-permute-start = (bf16[36,36,512]{2,1,0:T(8,128)(2,1)}, bf16[36,36,512]{2,1,0:T(8,128)(2,1)S(1)}, u32[]{:S(2)}, u32[]{:S(2)}) collective-permute-start(bf16[36,36,512]{2,1,0:T(8,128)(2,1)} %refs_1_.1), channel_id=1, source_target_pairs={{0,1},{1,0},{2,3},{3,2},{4,5},{5,4},{6,7},{7,6},{8,9},{9,8},{10,11... | collective-permute-start | bytes 3981320 | tf_op jit(solution)/shard_map/ppermute | solution.py:406
  24.7 45.7 %collective-permute-start.2 = (bf16[2,36,1152]{2,1,0:T(8,128)(2,1)S(1)}, bf16[2,36,1152]{2,1,0:T(8,128)(2,1)S(1)}, u32[]{:S(2)}, u32[]{:S(2)}) collective-permute-start(bf16[2,36,1152]{2,1,0:T(8,128)(2,1)S(1)} %collective-permute-done.1.refs_2_.refs_7_.refs_10_.refs_3_), channel_id=1, source_target_pairs={{0,1},{1,0},{2,3},{3,2},{4,5},{5,4},{6,7},{7,6},{8,9},{9,8},{10,11... | collective-permute-start | bytes 497672 | tf_op jit(solution)/shard_map/ppermute | solution.py:406
  24.8 45.6 %collective-permute-start.4 = (bf16[2,36,1152]{2,1,0:T(8,128)(2,1)S(1)}, bf16[2,36,1152]{2,1,0:T(8,128)(2,1)S(1)}, u32[]{:S(2)}, u32[]{:S(2)}) collective-permute-start(bf16[2,36,1152]{2,1,0:T(8,128)(2,1)S(1)} %collective-permute-done.3.refs_3_.refs_8_.refs_11_.refs_4_), channel_id=1, source_target_pairs={{0,1},{1,0},{2,3},{3,2},{4,5},{5,4},{6,7},{7,6},{8,9},{9,8},{10,11... | collective-permute-start | bytes 497672 | tf_op jit(solution)/shard_map/ppermute | solution.py:406
  26.7 2.1 %copy-start.1 = (bf16[4,20,1152]{2,1,0:T(8,128)(2,1)}, bf16[4,20,1152]{2,1,0:T(8,128)(2,1)S(1)}, u32[]{:S(2)}) copy-start(bf16[4,20,1152]{2,1,0:T(8,128)(2,1)S(1)} %collective-permute-done.7.refs_5_.refs_10_.refs_13_.refs_6_) | copy-start | bytes 552964
  26.7 43.7 %collective-permute-start.8 = (bf16[4,20,1152]{2,1,0:T(8,128)(2,1)S(1)}, bf16[4,20,1152]{2,1,0:T(8,128)(2,1)S(1)}, u32[]{:S(2)}, u32[]{:S(2)}) collective-permute-start(bf16[4,20,1152]{2,1,0:T(8,128)(2,1)S(1)} %collective-permute-done.7.refs_5_.refs_10_.refs_13_.refs_6_), channel_id=1, source_target_pairs={{0,1},{1,0},{2,3},{3,2},{4,5},{5,4},{6,7},{7,6},{8,9},{9,8},{10,11... | collective-permute-start | bytes 552968 | tf_op jit(solution)/shard_map/ppermute | solution.py:406
  26.8 2.0 %copy-start.2 = (bf16[4,20,1152]{2,1,0:T(8,128)(2,1)}, bf16[4,20,1152]{2,1,0:T(8,128)(2,1)S(1)}, u32[]{:S(2)}) copy-start(bf16[4,20,1152]{2,1,0:T(8,128)(2,1)S(1)} %collective-permute-done.5.refs_4_.refs_9_.refs_12_.refs_5_) | copy-start | bytes 552964
  26.8 43.6 %collective-permute-start.6 = (bf16[4,20,1152]{2,1,0:T(8,128)(2,1)S(1)}, bf16[4,20,1152]{2,1,0:T(8,128)(2,1)S(1)}, u32[]{:S(2)}, u32[]{:S(2)}) collective-permute-start(bf16[4,20,1152]{2,1,0:T(8,128)(2,1)S(1)} %collective-permute-done.5.refs_4_.refs_9_.refs_12_.refs_5_), channel_id=1, source_target_pairs={{0,1},{1,0},{2,3},{3,2},{4,5},{5,4},{6,7},{7,6},{8,9},{9,8},{10,11... | collective-permute-start | bytes 552968 | tf_op jit(solution)/shard_map/ppermute | solution.py:406
  70.4 0.7 copy-start.9
  70.4 0.7 copy-start.10
  70.4 0.8 copy-start.7
  70.5 0.8 copy-start.8
  70.5 1.3 copy-start
  109.6 37.0 %collective-permute-start.9 = (bf16[2,768,512]{2,1,0:T(8,128)(2,1)}, bf16[2,768,512]{2,1,0:T(8,128)(2,1)S(1)}, u32[]{:S(2)}, u32[]{:S(2)}) collective-permute-start(bf16[2,768,512]{2,1,0:T(8,128)(2,1)} %get-tuple-element.9.refs_1_), channel_id=1, source_target_pairs={{0,1},{1,0},{2,3},{3,2},{4,5},{5,4},{6,7},{7,6},{8,9},{9,8},{10,11... | collective-permute-start | bytes 4718600 | tf_op jit(solution)/shard_map/ppermute | solution.py:406
  146.6 1.2 copy-start.11

commit v5 on v4

--- a/solution.py
+++ b/solution.py
@@ -28,12 +28,13 @@
     for j in range(blocks):
         lanes = slice(LANES * j, LANES * j + LANES)
         for b in range(3):
-            wide_ref[b] = w_ref[0, b, :, :, lanes].astype(F32).reshape(depth * 4, LANES)
-        for gate in range(4):
-            out = slice(LANES * gate, LANES * gate + LANES)
-            for b in range(3):
-                rows = wide_ref[b, pl.ds(gate, depth, stride=4), :]
-                out_ref[j, depth * b : depth * b + depth, out] = rows.astype(BF16)
+            for c in range(0, depth, 32):
+                taken = w_ref[0, b, c : c + 32, :, lanes].astype(F32)
+                wide_ref[b, 4 * c : 4 * c + 128, :] = taken.reshape(128, LANES)
+                for gate in range(4):
+                    out = slice(LANES * gate, LANES * gate + LANES)
+                    rows = wide_ref[b, pl.ds(4 * c + gate, 32, stride=4), :]
+                    out_ref[j, depth * b + c : depth * b + c + 32, out] = rows.astype(BF16)
         out_ref[j, 3 * depth :, :] = jnp.zeros((depth, GATES), BF16)
 
 
@@ -312,9 +313,11 @@
         in_specs.append(whole(array) if spec is None else spec)
 
     args, in_specs, aliases = [], [], {}
-    for array in hiddens:
-        block = array.shape[:2] + (channels,)
-        add(array, pl.BlockSpec(block, lambda n, k: (0, 0, 0), pipeline_mode=once))
+    for place_of, array in enumerate(hiddens):
+        joined = place_of >= 3 and array.shape[0] == 8
+        block = (4 if joined else array.shape[0], array.shape[1], channels)
+        side = place_of - 3 if joined else 0
+        add(array, pl.BlockSpec(block, lambda n, k, side=side: (side, 0, 0), pipeline_mode=once))
     if first:
         inner, *rims, w_in, biases = frame
         add(inner)
@@ -453,7 +456,11 @@
     if paired:
         me = lax.axis_index("ch").astype(jnp.int32)
         halves = (me, 1 - me)
-        hiddens = ((hidden_init, *rims), (other, *[swapped(rim) for rim in rims]))
+        sides = swapped(jnp.concatenate([west, east]))
+        hiddens = (
+            (hidden_init, *rims),
+            (other, swapped(north), swapped(south), sides, sides),
+        )
     else:
         halves = (jnp.int32(0), jnp.int32(1))
         full = [other] + [gather(rim[:, :, :width]) for rim in rims]

time: 176 us -> 174 us (0.989)
  starting transfers between devices: 16.3 us -> 14.5 us
    ppermute x6 -> x5, waiting for transfers between devices: 4.64 us -> 2.93 us  [swapped(): return lax.ppermute(x, 'ch', [(0, 1), (1, 0)])]
    ppermute x6 -> x5, starting transfers between devices: 6.71 us -> 5.53 us  [swapped(): return lax.ppermute(x, 'ch', [(0, 1), (1, 0)])]
  transfers between devices with their start and end apart: 10 -> 9, of which waited for: 2 -> 2; matrix products, arithmetic and copies ran while one was open for 2% -> 3% of each run, Pallas kernels for 44% -> 45%
where the time goes in v5:
time: 174 us; the launch traced here: 173 us
  Pallas kernels  144 us (83%)
  starting transfers between devices  14.5 us (8%)
  local copies, waits for them, and re-layouts  8.79 us (5%)
  waiting for transfers between devices  3.29 us (2%)
    pallas_call x4, Pallas kernels, run_pass(): pl.pallas_call(functools.partial(pass_kernel, dims), grid_spec=pltpu.Pref...  139 us
    ppermute x2, starting transfers between devices, forward(): return lax.ppermute(x, axis, [(i, i + 1) for i in range(count - 1)])  6.36 us
    ppermute x5, starting transfers between devices, swapped(): return lax.ppermute(x, 'ch', [(0, 1), (1, 0)])  5.53 us
    pallas_call x1, Pallas kernels, input_weights(): pl.pallas_call(functools.partial(input_weights_kernel, depth, blocks), gr...  4.51 us
  transfers between devices with their start and end apart: 9, of which 2 were waited for; matrix products, arithmetic and copies ran while one was open for 3% of the time, Pallas kernels for 45%

profile of v5, /device:TPU:0, one launch (start us, length us, event | category | flops | bytes accessed | tf_op | source)
XLA Modules:
  0.0 172.6 jit_solution(7567647926652070607)
XLA Ops:
  0.6 0.8 fusion.16
  1.4 0.9 reduce-precision_convert_fusion.2
  2.3 0.9 fusion.14
  3.3 2.4 %collective-permute-start.1 = (bf16[2,36,1152]{2,1,0:T(8,128)(2,1)S(1)}, bf16[2,36,1152]{2,1,0:T(8,128)(2,1)S(1)}, u32[]{:S(2)}, u32[]{:S(2)}) collective-permute-start(bf16[2,36,1152]{2,1,0:T(8,128)(2,1)S(1)} %maximum_maximum_fusion), channel_id=1, source_target_pairs={{0,8},{8,16},{16,24},{1,9},{9,17},{17,25},{2,10},{10,18},{18,26},{... | collective-permute-start | bytes 497672 | tf_op jit(solution)/shard_map/ppermute | solution.py:400
  5.7 1.3 collective-permute-start.3
  7.0 1.0 fusion.15
  8.0 1.4 fusion.12
  9.3 1.2 fusion.13
  10.6 0.0 collective-permute-done.1.refs_2_.refs_7_.refs_10_.refs_3_
  10.6 0.0 copy-start.6
  10.8 0.3 collective-permute-done.3.refs_3_.refs_8_.refs_11_.refs_4_
  11.1 0.0 copy-start.7
  11.2 0.1 pad_maximum_fusion.1
  11.3 0.1 reshape.22
  11.4 0.1 pad_maximum_fusion.2
  11.5 0.1 reshape.24
  11.6 0.0 copy-start.4
  11.6 0.0 copy-start.5
  11.7 4.0 %collective-permute-start.5 = (bf16[4,20,1152]{2,1,0:T(8,128)(2,1)S(1)}, bf16[4,20,1152]{2,1,0:T(8,128)(2,1)S(1)}, u32[]{:S(2)}, u32[]{:S(2)}) collective-permute-start(bf16[4,20,1152]{2,1,0:T(8,128)(2,1)S(1)} %bitcast.31), channel_id=1, source_target_pairs={{0,2},{2,4},{4,6},{1,3},{3,5},{5,7},{8,10},{10,12},{12,14},{9,11},... | collective-permute-start | bytes 552968 | tf_op jit(solution)/shard_map/ppermute | solution.py:400
  15.7 1.3 collective-permute-start.6
  17.0 1.6 collective-permute-start
  18.5 0.6 stack.63.refs_0_
  19.2 0.0 copy-done.4
  19.2 0.0 copy-done.5
  19.2 4.5 %input_weights.1.refs_11_.refs_7_ = bf16[4,768,512]{2,1,0:T(8,128)(2,1)} custom-call(bf16[3,3,64,4,512]{4,3,2,1,0:T(4,128)(2,1)} %bitcast.28, bf16[4,20,1152]{2,1,0:T(8,128)(2,1)} %bitcast.32, bf16[4,20,1152]{2,1,0:T(8,128)(2,1)} %bitcast.30), custom_call_target="tpu_custom_call" | custom-call | bytes 6291456 | tf_op jit(solution)/shard_map/input_weights/pallas_call | solution.py:44
  23.7 0.0 copy-done.6
  23.7 0.5 collective-permute-start.2
  24.2 0.0 copy-done.7
  24.2 1.5 collective-permute-start.4
  25.7 0.0 collective-permute-done.5.refs_4_.refs_9_.refs_12_.refs_5_
  25.7 0.0 copy-start
  25.7 0.0 collective-permute-done.6.refs_5_.refs_10_.refs_13_.refs_6_
  25.7 0.0 copy-start.1
  25.7 0.1 pad_maximum_fusion
  25.8 0.6 collective-permute-start.7
  26.4 0.0 copy-done
  26.4 0.1 copy-done.1
  26.5 41.6 %step0.2 = (f32[4,2,768,512]{3,2,1,0:T(8,128)}, bf16[4,2,2,3,1024,512]{5,4,3,2,1,0:T(8,128)(2,1)}) custom-call(s32[6]{0:T(128)} %stack.63.refs_0_, bf16[36,36,512]{2,1,0:T(8,128)(2,1)} %refs_1_.1, bf16[2,36,1152]{2,1,0:T(8,128)(2,1)} %copy-done.6, bf16[2,36,1152]{2,1,0:T(8,128)(2,1)} %copy-done.7, bf16[4,20,1152]{2,1,0:T(8,128)(2,1)} %copy-done, ...), custom_call_target="tpu_custom_call" | custom-call | flops 19327352832 | bytes 25165824 | tf_op jit(solution)/shard_map/step0/pallas_call | solution.py:377
  68.1 0.0 collective-permute-done.2.refs_2_
  68.1 0.0 copy-start.8
  68.1 0.0 collective-permute-done.4.refs_3_
  68.1 0.0 copy-start.9
  68.1 0.0 collective-permute-done.7.refs_4_.refs_5_
  68.2 0.0 copy-start.2
  68.2 0.0 collective-permute-done.refs_1_
  68.2 0.0 copy-start.3
  68.2 0.6 copy-done.8
  68.8 0.1 copy-done.9
  68.9 0.2 copy-done.2
  69.0 0.5 copy-done.3
  69.5 37.8 %step0.3 = (bf16[2,768,512]{2,1,0:T(8,128)(2,1)}, f32[4,2,768,128]{3,2,1,0:T(8,128)}, bf16[4,2,2,3,1024,512]{5,4,3,2,1,0:T(8,128)(2,1)}) custom-call(s32[6]{0:T(128)} %stack.63.refs_0_, bf16[36,36,512]{2,1,0:T(8,128)(2,1)} %copy-done.3, bf16[2,36,1152]{2,1,0:T(8,128)(2,1)} %copy-done.8, ...), custom_call_target="tpu_custom_call", output_to_operand_aliasing={{2}: (8, {})} | custom-call | flops 19327352832 | bytes 25165824 | tf_op jit(solution)/shard_map/step0/pallas_call | solution.py:377
  107.3 1.3 collective-permute-start.8
  108.6 31.8 %step1.2.refs_2_ = f32[4,2,720,512]{3,2,1,0:T(8,128)} custom-call(s32[6]{0:T(128)} %stack.63.refs_0_, bf16[2,768,512]{2,1,0:T(8,128)(2,1)} %get-tuple-element.9.refs_1_, bf16[36,36,128]{2,1,0:T(8,128)(2,1)} %refs_2_.1, bf16[2,36,1152]{2,1,0:T(8,128)(2,1)} %copy-done.6, bf16[2,36,1152]{2,1,0:T(8,128)(2,1)} %copy-done.7, bf16[4,20,1152]{2,1,0:T(8,128)(2,1)} %copy-done, ...), custom_call_target="tpu_custom_call" | custom-call | flops 18119393280 | bytes 25165824 | tf_op jit(solution)/shard_map/step1/pallas_call | solution.py:377
  140.4 2.9 %collective-permute-done.8.refs_1_ = bf16[2,768,512]{2,1,0:T(8,128)(2,1)S(1)} collective-permute-done((bf16[2,768,512]{2,1,0:T(8,128)(2,1)}, bf16[2,768,512]{2,1,0:T(8,128)(2,1)S(1)}, u32[]{:S(2)}, u32[]{:S(2)}) %collective-permute-start.8) | collective-permute-done | bytes 1572896 | tf_op jit(solution)/shard_map/ppermute | solution.py:409
  143.3 0.0 copy-start.10
  143.3 1.2 copy-done.10
  144.5 28.2 %step1.3 = (bf16[36,36,512]{2,1,0:T(8,128)(2,1)}, f32[36,36,512]{2,1,0:T(8,128)}) custom-call(s32[6]{0:T(128)} %stack.63.refs_0_, bf16[2,768,512]{2,1,0:T(8,128)(2,1)} %copy-done.10, f32[4,2,720,512]{3,2,1,0:T(8,128)} %step1.2.refs_2_, bf16[4,2,2,3,1024,512]{5,4,3,2,1,0:T(8,128)(2,1)} %get-tuple-element.10.refs_9_.refs_3_, ...), custom_call_target="tpu_custom_call" | custom-call | flops 18119393280 | bytes 25165824 | tf_op jit(solution)/shard_map/step1/pallas_call | solution.py:377
  (23 shorter events, 0.3 us)
Async XLA Ops:
  3.3 7.3 %collective-permute-start.1 = (bf16[2,36,1152]{2,1,0:T(8,128)(2,1)S(1)}, bf16[2,36,1152]{2,1,0:T(8,128)(2,1)S(1)}, u32[]{:S(2)}, u32[]{:S(2)}) collective-permute-start(bf16[2,36,1152]{2,1,0:T(8,128)(2,1)S(1)} %maximum_maximum_fusion), channel_id=1, source_target_pairs={{0,8},{8,16},{16,24},{1,9},{9,17},{17,25},{2,10},{10,18},{18,26},{... | collective-permute-start | bytes 497672 | tf_op jit(solution)/shard_map/ppermute | solution.py:400
  5.7 5.4 %collective-permute-start.3 = (bf16[2,36,1152]{2,1,0:T(8,128)(2,1)S(1)}, bf16[2,36,1152]{2,1,0:T(8,128)(2,1)S(1)}, u32[]{:S(2)}, u32[]{:S(2)}) collective-permute-start(bf16[2,36,1152]{2,1,0:T(8,128)(2,1)S(1)} %maximum_maximum_fusion.1), channel_id=1, source_target_pairs={{8,0},{16,8},{24,16},{9,1},{17,9},{25,17},{10,2},{18,10},{26,18},{... | collective-permute-start | bytes 497672 | tf_op jit(solution)/shard_map/ppermute | solution.py:405
  10.6 13.0 %copy-start.6 = (bf16[2,36,1152]{2,1,0:T(8,128)(2,1)}, bf16[2,36,1152]{2,1,0:T(8,128)(2,1)S(1)}, u32[]{:S(2)}) copy-start(bf16[2,36,1152]{2,1,0:T(8,128)(2,1)S(1)} %collective-permute-done.1.refs_2_.refs_7_.refs_10_.refs_3_) | copy-start | bytes 497668
  11.1 13.1 %copy-start.7 = (bf16[2,36,1152]{2,1,0:T(8,128)(2,1)}, bf16[2,36,1152]{2,1,0:T(8,128)(2,1)S(1)}, u32[]{:S(2)}) copy-start(bf16[2,36,1152]{2,1,0:T(8,128)(2,1)S(1)} %collective-permute-done.3.refs_3_.refs_8_.refs_11_.refs_4_) | copy-start | bytes 497668
  11.6 7.6 %copy-start.4 = (bf16[20,2,2,1152]{3,0,1,2:T(8,128)(2,1)}, bf16[20,2,2,1152]{3,0,1,2:T(8,128)(2,1)S(1)}, u32[]{:S(2)}) copy-start(bf16[20,2,2,1152]{3,0,1,2:T(8,128)(2,1)S(1)} %copy.24) | copy-start | bytes 552964
  11.6 7.5 %copy-start.5 = (bf16[20,2,2,1152]{3,0,1,2:T(8,128)(2,1)}, bf16[20,2,2,1152]{3,0,1,2:T(8,128)(2,1)S(1)}, u32[]{:S(2)}) copy-start(bf16[20,2,2,1152]{3,0,1,2:T(8,128)(2,1)S(1)} %copy.18) | copy-start | bytes 552964
  11.7 14.1 %collective-permute-start.5 = (bf16[4,20,1152]{2,1,0:T(8,128)(2,1)S(1)}, bf16[4,20,1152]{2,1,0:T(8,128)(2,1)S(1)}, u32[]{:S(2)}, u32[]{:S(2)}) collective-permute-start(bf16[4,20,1152]{2,1,0:T(8,128)(2,1)S(1)} %bitcast.31), channel_id=1, source_target_pairs={{0,2},{2,4},{4,6},{1,3},{3,5},{5,7},{8,10},{10,12},{12,14},{9,11},... | collective-permute-start | bytes 552968 | tf_op jit(solution)/shard_map/ppermute | solution.py:400
  15.7 10.1 %collective-permute-start.6 = (bf16[4,20,1152]{2,1,0:T(8,128)(2,1)S(1)}, bf16[4,20,1152]{2,1,0:T(8,128)(2,1)S(1)}, u32[]{:S(2)}, u32[]{:S(2)}) collective-permute-start(bf16[4,20,1152]{2,1,0:T(8,128)(2,1)S(1)} %bitcast.29), channel_id=1, source_target_pairs={{2,0},{4,2},{6,4},{3,1},{5,3},{7,5},{10,8},{12,10},{14,12},{11,9},... | collective-permute-start | bytes 552968 | tf_op jit(solution)/shard_map/ppermute | solution.py:405
  17.0 51.2 %collective-permute-start = (bf16[36,36,512]{2,1,0:T(8,128)(2,1)}, bf16[36,36,512]{2,1,0:T(8,128)(2,1)S(1)}, u32[]{:S(2)}, u32[]{:S(2)}) collective-permute-start(bf16[36,36,512]{2,1,0:T(8,128)(2,1)} %refs_1_.1), channel_id=1, source_target_pairs={{0,1},{1,0},{2,3},{3,2},{4,5},{5,4},{6,7},{7,6},{8,9},{9,8},{10,11... | collective-permute-start | bytes 3981320 | tf_op jit(solution)/shard_map/ppermute | solution.py:409
  23.7 44.4 %collective-permute-start.2 = (bf16[2,36,1152]{2,1,0:T(8,128)(2,1)S(1)}, bf16[2,36,1152]{2,1,0:T(8,128)(2,1)S(1)}, u32[]{:S(2)}, u32[]{:S(2)}) collective-permute-start(bf16[2,36,1152]{2,1,0:T(8,128)(2,1)S(1)} %collective-permute-done.1.refs_2_.refs_7_.refs_10_.refs_3_), channel_id=1, source_target_pairs={{0,1},{1,0},{2,3},{3,2},{4,5},{5,4},{6,7},{7,6},{8,9},{9,8},{10,11... | collective-permute-start | bytes 497672 | tf_op jit(solution)/shard_map/ppermute | solution.py:409
  24.2 43.9 %collective-permute-start.4 = (bf16[2,36,1152]{2,1,0:T(8,128)(2,1)S(1)}, bf16[2,36,1152]{2,1,0:T(8,128)(2,1)S(1)}, u32[]{:S(2)}, u32[]{:S(2)}) collective-permute-start(bf16[2,36,1152]{2,1,0:T(8,128)(2,1)S(1)} %collective-permute-done.3.refs_3_.refs_8_.refs_11_.refs_4_), channel_id=1, source_target_pairs={{0,1},{1,0},{2,3},{3,2},{4,5},{5,4},{6,7},{7,6},{8,9},{9,8},{10,11... | collective-permute-start | bytes 497672 | tf_op jit(solution)/shard_map/ppermute | solution.py:409
  25.7 0.7 copy-start
  25.7 0.8 copy-start.1
  25.8 42.3 %collective-permute-start.7 = (bf16[8,20,1152]{2,1,0:T(8,128)(2,1)S(1)}, bf16[8,20,1152]{2,1,0:T(8,128)(2,1)S(1)}, u32[]{:S(2)}, u32[]{:S(2)}) collective-permute-start(bf16[8,20,1152]{2,1,0:T(8,128)(2,1)S(1)} %pad_maximum_fusion), channel_id=1, source_target_pairs={{0,1},{1,0},{2,3},{3,2},{4,5},{5,4},{6,7},{7,6},{8,9},{9,8},{10,11... | collective-permute-start | bytes 1105928 | tf_op jit(solution)/shard_map/ppermute | solution.py:409
  68.1 0.7 copy-start.8
  68.1 0.7 copy-start.9
  68.2 0.9 copy-start.2
  68.2 1.3 copy-start.3
  107.3 36.0 %collective-permute-start.8 = (bf16[2,768,512]{2,1,0:T(8,128)(2,1)}, bf16[2,768,512]{2,1,0:T(8,128)(2,1)S(1)}, u32[]{:S(2)}, u32[]{:S(2)}) collective-permute-start(bf16[2,768,512]{2,1,0:T(8,128)(2,1)} %get-tuple-element.9.refs_1_), channel_id=1, source_target_pairs={{0,1},{1,0},{2,3},{3,2},{4,5},{5,4},{6,7},{7,6},{8,9},{9,8},{10,11... | collective-permute-start | bytes 4718600 | tf_op jit(solution)/shard_map/ppermute | solution.py:409
  143.3 1.2 copy-start.10
